TPU v7x, 32 devices: a whole 2x2x4 slice. The times are simulated.
32 devices in a mesh: rep: 2 (over y), steal: 4 (over x, core), ep: 4 (over z).
Axes of the slice: x: 2, y: 2, z: 4, core: 2. Of those that a mesh axis runs over, the one named last changes fastest.
Arguments:
- queries: bfloat16 [512, 128, 576], P(('rep', 'steal', 'ep')), parts along dimension 0
- latent_cache: bfloat16 [512, 128, 576], P(('rep', 'steal', 'ep')), parts along dimension 0
- cache_length: int32 [512], P(('rep', 'steal', 'ep')), parts along dimension 0, may hold values from 16 to 128, as said below
- steal_source: int32 [512], P(('rep', 'steal', 'ep')), parts along dimension 0, may hold values from 0 to 3, as said below
- hidden: bfloat16 [512, 7168], P(('rep', 'steal', 'ep')), parts along dimension 0
- norm_gain: float32 [7168], replicated, may hold values from 0.1 to 1.9
- expert_ids: int32 [512, 2], P(('rep', 'steal', 'ep')), parts along dimension 0, may hold values from 0 to 3, all different within a row; in each aligned block of 16 rows (0 to 15, 16 to 31, ...) at most 12 rows name the same one
- expert_weight: float32 [512, 2], P(('rep', 'steal', 'ep')), parts along dimension 0, may hold values from 0.05 to 0.45
- w_gate: bfloat16 [4, 7168, 1024], P('ep', 'steal'), may hold values from -0.0625 to 0.0625
- w_up: bfloat16 [4, 7168, 1024], P('ep', 'steal'), may hold values from -0.0625 to 0.0625
- w_down: bfloat16 [4, 1024, 7168], P('ep', None, 'steal'), may hold values from -0.1875 to 0.1875
Outputs:
- attended: bfloat16 [512, 128, 512], P(('rep', 'steal', 'ep')), parts along dimension 0
- mixed: bfloat16 [512, 7168], P(('rep', 'steal', 'ep')), parts along dimension 0
There are 2 independent parts, one for each index of `rep`. A program takes and returns all parts, laid end to end along the dimension named above; an argument that names none is the same for every part. Nothing has to cross between parts.
Inputs may be any that keep to these rules, and one draw needn't show every extreme that they name: Slots 3 and later of every device serve the device's own request (steal_source equals the device's steal index). For a slot j below 3 and one ep index, all devices along steal share one offset o in 1 to 3 with steal_source = (steal index - o) mod 4, and the 3 slots of an ep index have distinct offsets. `cache_length`: every device serves a request with exactly 128 valid positions. `expert_ids`: the rows of one device name one expert at most 12 times.
All inputs are finite; a program needn't handle non-finite values.
Results may differ from a plain program's by a relative error of at most 0.019.
Values may be sent and summed in bfloat16 or wider, within the bound.
No kernel may reach another device: no remote copies, remote signals or barrier semaphores. Data moves between devices by JAX's collectives and lax.ppermute only.
A program may use at most 128 MiB of HBM per device.

v0:
```python
import jax
import jax.numpy as jnp
from jax import lax
from jax.sharding import PartitionSpec as P

LAT = 512


score_scale = 192.0 ** (-0.5)
norm_eps = 1e-06


def attend_served(served_queries, served_cache, cache_length):
    scores = (
        jnp.einsum("rhc,rtc->rht", served_queries, served_cache, preferred_element_type=jnp.float32)
        * score_scale
    )
    places = jnp.arange(served_cache.shape[1], dtype=jnp.int32)
    valid = places[None, None, :] < cache_length[:, None, None]
    scores = jnp.where(valid, scores, -jnp.inf)
    peak = jnp.max(scores, axis=-1, keepdims=True)
    raised = jnp.exp(scores - peak)
    probs = (raised / jnp.sum(raised, axis=-1, keepdims=True)).astype(jnp.bfloat16)
    output = jnp.einsum(
        "rht,rtc->rhc", probs, served_cache[:, :, :LAT], preferred_element_type=jnp.float32
    )
    return output.astype(jnp.bfloat16)


def per_device(
    queries,
    latent_cache,
    cache_length,
    steal_source,
    hidden,
    norm_gain,
    expert_ids,
    expert_weight,
    w_gate,
    w_up,
    w_down,
):
    here = lax.axis_index("steal")
    width = lax.axis_size("steal")
    requests = queries.shape[0]
    offset = (here - steal_source) % width
    target = (here + offset) % width
    peers = jnp.arange(width, dtype=jnp.int32)
    lent = offset != 0
    send_map = ((target[None, :] == peers[:, None]) & lent[None, :]).astype(jnp.bfloat16)
    query_rows = queries.reshape(requests, -1)
    cache_rows = latent_cache.reshape(requests, -1)
    send_queries = jnp.dot(send_map, query_rows, preferred_element_type=jnp.float32).astype(
        jnp.bfloat16
    )
    send_caches = jnp.dot(send_map, cache_rows, preferred_element_type=jnp.float32).astype(
        jnp.bfloat16
    )
    got_queries, got_caches = (
        lax.all_to_all(send_queries, "steal", split_axis=0, concat_axis=0, tiled=True),
        lax.all_to_all(send_caches, "steal", split_axis=0, concat_axis=0, tiled=True),
    )
    take_map = ((steal_source[:, None] == peers[None, :]) & lent[:, None]).astype(jnp.bfloat16)
    taken_queries = jnp.dot(take_map, got_queries, preferred_element_type=jnp.float32).astype(
        jnp.bfloat16
    )
    taken_caches = jnp.dot(take_map, got_caches, preferred_element_type=jnp.float32).astype(
        jnp.bfloat16
    )
    served_queries = jnp.where(lent[:, None], taken_queries, query_rows).reshape(queries.shape)
    served_cache = jnp.where(lent[:, None], taken_caches, cache_rows).reshape(latent_cache.shape)
    attended = attend_served(served_queries, served_cache, cache_length)
    values = hidden.astype(jnp.float32)
    scale = lax.rsqrt(jnp.mean(values * values, axis=-1, keepdims=True) + norm_eps)
    normed = (values * scale * norm_gain).astype(jnp.bfloat16)
    model_width = normed.shape[1]
    slice_width = model_width // width
    experts = lax.axis_size("ep")
    top = expert_ids.shape[1]
    room = requests * top // experts * 3 // 2
    flat_ids = expert_ids.reshape(-1)
    hits = (flat_ids[:, None] == jnp.arange(experts, dtype=jnp.int32)[None, :]).astype(jnp.int32)
    before = jnp.cumsum(hits, axis=0) - hits
    place = jnp.sum(before * hits, axis=1)
    slot = flat_ids * room + place
    matches = slot[None, :] == jnp.arange(experts * room, dtype=jnp.int32)[:, None]
    token_map = jnp.sum(matches.astype(jnp.bfloat16).reshape(experts, room, requests, top), axis=-1)
    normed_slices = normed.reshape(requests, width, slice_width)
    outgoing = jnp.einsum(
        "xqr,rsk->xsqk", token_map, normed_slices, preferred_element_type=jnp.float32
    ).astype(jnp.bfloat16)
    by_expert = lax.all_to_all(outgoing, "ep", split_axis=0, concat_axis=0, tiled=True)
    arrived = lax.all_to_all(by_expert, "steal", split_axis=1, concat_axis=1, tiled=True)
    expert_rows = arrived.reshape(-1, slice_width)
    gate_part = (
        jnp.dot(expert_rows, w_gate[0], preferred_element_type=jnp.float32)
        .astype(jnp.bfloat16)
        .astype(jnp.float32)
    )
    up_part = (
        jnp.dot(expert_rows, w_up[0], preferred_element_type=jnp.float32)
        .astype(jnp.bfloat16)
        .astype(jnp.float32)
    )
    gate_sum, up_sum = (
        lax.psum(gate_part.astype(jnp.bfloat16), "steal").astype(jnp.float32),
        lax.psum(up_part.astype(jnp.bfloat16), "steal").astype(jnp.float32),
    )
    activated = (jax.nn.silu(gate_sum) * up_sum).astype(jnp.bfloat16)
    produced = jnp.dot(activated, w_down[0], preferred_element_type=jnp.float32).astype(
        jnp.bfloat16
    )
    produced = produced.reshape(arrived.shape)
    returned = lax.all_to_all(
        lax.all_to_all(produced, "steal", split_axis=1, concat_axis=1, tiled=True),
        "ep",
        split_axis=0,
        concat_axis=0,
        tiled=True,
    )
    weight_map = jnp.sum(
        (matches.astype(jnp.float32) * expert_weight.reshape(-1)[None, :]).reshape(
            experts, room, requests, top
        ),
        axis=-1,
    )
    mixed = jnp.einsum(
        "xqr,xsqk->rsk",
        weight_map,
        returned.astype(jnp.float32),
        precision=lax.Precision.HIGHEST,
        preferred_element_type=jnp.float32,
    )
    mixed = mixed.reshape(requests, model_width).astype(jnp.bfloat16)
    return (attended, mixed)


def solution(mesh):
    return jax.shard_map(
        per_device,
        mesh=mesh,
        in_specs=(
            P(("rep", "steal", "ep"), None, None),
            P(("rep", "steal", "ep"), None, None),
            P(("rep", "steal", "ep")),
            P(("rep", "steal", "ep")),
            P(("rep", "steal", "ep"), None),
            P(),
            P(("rep", "steal", "ep"), None),
            P(("rep", "steal", "ep"), None),
            P("ep", "steal", None),
            P("ep", "steal", None),
            P("ep", None, "steal"),
        ),
        out_specs=(P(("rep", "steal", "ep"), None, None), P(("rep", "steal", "ep"), None)),
        check_vma=False,
    )
```

profile of v0, /device:TPU:17, one launch (start us, length us, event | category | flops | bytes accessed | tf_op | source)
XLA Modules:
  0.0 161.6 jit_solution(14712808303742314024)
XLA Ops:
  13.4 4.8 %all-to-all-start.2 = ((bf16[4,4,12,1792]{3,1,2,0:T(4,128)(2,1)}), bf16[4,4,12,1792]{3,1,2,0:T(4,128)(2,1)S(1)}, u32[]{:S(2)}, u32[]{:S(2)}) async-start(bf16[4,4,12,1792]{3,1,2,0:T(4,128)(2,1)} %copy.107), calls=%async_computation.2 | async-start | bytes 1376256 | tf_op jit(solution)/shard_map/all_to_all | solution.py:92
  18.2 14.5 %all-to-all-done.2 = bf16[4,4,12,1792]{3,1,2,0:T(4,128)(2,1)S(1)} async-done(((bf16[4,4,12,1792]{3,1,2,0:T(4,128)(2,1)}), bf16[4,4,12,1792]{3,1,2,0:T(4,128)(2,1)S(1)}, u32[]{:S(2)}, u32[]{:S(2)}) %all-to-all-start.2) | async-done | bytes 688160 | tf_op jit(solution)/shard_map/all_to_all | solution.py:92
  33.9 4.9 %all-to-all-start.3 = ((bf16[4,4,12,1792]{3,0,2,1:T(4,128)(2,1)}), bf16[4,4,12,1792]{3,0,2,1:T(4,128)(2,1)S(1)}, u32[]{:S(2)}, u32[]{:S(2)}) async-start(bf16[4,4,12,1792]{3,0,2,1:T(4,128)(2,1)} %copy.108), calls=%async_computation.3 | async-start | bytes 1376256 | tf_op jit(solution)/shard_map/all_to_all | solution.py:93
  38.8 4.3 %copy.98 = bf16[16,128,576]{2,1,0:T(8,128)(2,1)} copy(bf16[16,128,576]{1,2,0:T(8,128)(2,1)} %param.12) | data formatting | bytes 4718592 | tf_op args[1]
  43.2 4.4 %reshape.109 = bf16[16,73728]{1,0:T(8,128)(2,1)S(1)} reshape(bf16[16,128,576]{2,1,0:T(8,128)(2,1)} %copy.98) | data formatting | bytes 4718592 | tf_op jit(solution)/shard_map/reshape | solution.py:52
  49.4 3.2 %reduce.1 = bf16[4,73728]{1,0:T(4,128)(2,1)} reduce(bf16[4,1,73728]{2,0,1:T(4,128)(2,1)} %fusion.4, bf16[]{:T(256)} %broadcast.99), dimensions={1}, to_apply=%copy.99.reduce_sub_computation | reduce | bytes 1179650 | tf_op jit(solution)/shard_map/all_to_all | solution.py:61
  52.6 2.5 %reshape.118 = bf16[4,2,36864]{2,1,0:T(2,128)(2,1)} reshape(bf16[4,73728]{1,0:T(4,128)(2,1)} %reduce.1) | data formatting | bytes 1179648
  55.1 4.2 %all-to-all-start.1 = ((bf16[4,2,36864]{2,1,0:T(2,128)(2,1)}), bf16[4,2,36864]{2,1,0:T(2,128)(2,1)}, u32[]{:S(2)}, u32[]{:S(2)}) async-start(bf16[4,2,36864]{2,1,0:T(2,128)(2,1)} %reshape.118), calls=%async_computation.1 | async-start | bytes 1179648 | tf_op jit(solution)/shard_map/all_to_all | solution.py:61
  61.6 4.0 %fusion.24 = bf16[192,1024]{1,0:T(8,128)(2,1)} fusion(bf16[192,1792]{1,0:T(8,128)(2,1)} %reshape.112, bf16[1,1792,1024]{2,1,0:T(8,128)(2,1)} %param.19), kind=kOutput, calls=%fused_computation.27 | convolution fusion | flops 704839680 | bytes 4751360 | tf_op jit(solution)/shard_map/dot_general | solution.py:96
  67.3 4.3 %copy.96 = bf16[16,128,576]{2,1,0:T(8,128)(2,1)} copy(bf16[16,128,576]{1,2,0:T(8,128)(2,1)} %param.11) | data formatting | bytes 4718592 | tf_op args[0]
  71.6 5.4 %reshape.107 = bf16[16,73728]{1,0:T(8,128)(2,1)} reshape(bf16[16,128,576]{2,1,0:T(8,128)(2,1)} %copy.96) | data formatting | bytes 4718592 | tf_op jit(solution)/shard_map/reshape | solution.py:51
  82.0 4.3 %all-to-all-start = ((bf16[4,2,36864]{2,1,0:T(2,128)(2,1)}), bf16[4,2,36864]{2,1,0:T(2,128)(2,1)}, u32[]{:S(2)}, u32[]{:S(2)}) async-start(bf16[4,2,36864]{2,1,0:T(2,128)(2,1)} %reshape.120), calls=%async_computation | async-start | bytes 1179648 | tf_op jit(solution)/shard_map/all_to_all | solution.py:60
  86.3 16.5 %all-reduce.3.cloned.1.call-done = (bf16[192,1024]{1,0:T(8,128)(2,1)}, bf16[192,1024]{1,0:T(8,128)(2,1)}) async-done(((bf16[192,1024]{1,0:T(8,128)(2,1)}, bf16[192,1024]{1,0:T(8,128)(2,1)}), (bf16[192,1024]{1,0:T(8,128)(2,1)}, bf16[192,1024]{1,0:T(8,128)(2,1)})) %all-reduce.3.cloned.1.call-update) | async-done | bytes 786448 | tf_op jit(solution)/shard_map/psum | solution.py:107
  102.8 4.1 %fusion.12 = bf16[192,1792]{1,0:T(8,128)(2,1)} fusion(bf16[1,1024,1792]{2,1,0:T(8,128)(2,1)} %param.21, bf16[192,1024]{1,0:T(8,128)(2,1)} %get-tuple-element.2, bf16[192,1024]{1,0:T(8,128)(2,1)} %get-tuple-element.3), kind=kOutput, calls=%fused_computation.18 | convolution fusion | flops 706560000 | bytes 5144576 | tf_op jit(solution)/shard_map/dot_general | solution.py:110
  109.7 5.3 %all-to-all-start.4 = ((bf16[4,4,12,1792]{3,0,2,1:T(4,128)(2,1)}), bf16[4,4,12,1792]{3,0,2,1:T(4,128)(2,1)S(1)}, u32[]{:S(2)}, u32[]{:S(2)}) async-start(bf16[4,4,12,1792]{3,0,2,1:T(4,128)(2,1)} %copy.110), calls=%async_computation.4 | async-start | bytes 1376256 | tf_op jit(solution)/shard_map/all_to_all | solution.py:115
  115.1 3.5 %reshape.119 = bf16[4,1,73728]{2,1,0:T(2,128)(2,1)} reshape(bf16[4,2,36864]{2,1,0:T(2,128)(2,1)} %all-to-all-done.1) | data formatting | bytes 1179648
  118.7 3.5 %reshape.121 = bf16[4,1,73728]{2,1,0:T(2,128)(2,1)} reshape(bf16[4,2,36864]{2,1,0:T(2,128)(2,1)} %all-to-all-done) | data formatting | bytes 1179648
  122.2 3.6 %fusion.2 = bf16[16,73728]{1,0:T(8,128)(2,1)} fusion(bf16[16,73728]{1,0:T(8,128)(2,1)S(1)} %reshape.109, pred[16]{0:T(512)(128)(4,1)S(1)} %broadcast_compare_fusion, bf16[4,1,73728]{2,1,0:T(2,128)(2,1)} %reshape.119, s32[16]{0:T(128)S(1)} %copy-done.5), kind=kOutput, calls=%fused_computation.4 | convolution fusion | flops 11796608 | bytes 5308496 | tf_op jit(solution)/shard_map/dot_general | solution.py:67
  127.1 5.1 %all-to-all-start.5 = ((bf16[4,4,12,1792]{3,1,2,0:T(4,128)(2,1)}), bf16[4,4,12,1792]{3,1,2,0:T(4,128)(2,1)S(1)}, u32[]{:S(2)}, u32[]{:S(2)}) async-start(bf16[4,4,12,1792]{3,1,2,0:T(4,128)(2,1)} %copy.111), calls=%async_computation.5 | async-start | bytes 1376256 | tf_op jit(solution)/shard_map/all_to_all | solution.py:114
  132.2 3.6 %fusion.1 = bf16[16,73728]{1,0:T(8,128)(2,1)} fusion(bf16[16,73728]{1,0:T(8,128)(2,1)S(1)} %copy-done, pred[16]{0:T(512)(128)(4,1)S(1)} %broadcast_compare_fusion, bf16[4,1,73728]{2,1,0:T(2,128)(2,1)} %reshape.121, s32[16]{0:T(128)S(1)} %copy-done.5), kind=kOutput, calls=%fused_computation.3 | convolution fusion | flops 11796608 | bytes 5308496 | tf_op jit(solution)/shard_map/dot_general | solution.py:64
  135.8 4.4 %reshape.110 = bf16[16,128,576]{2,1,0:T(8,128)(2,1)S(1)} reshape(bf16[16,73728]{1,0:T(8,128)(2,1)} %fusion.2) | data formatting | bytes 4718592 | tf_op jit(solution)/shard_map/reshape | solution.py:71
  140.2 5.5 %reshape.108 = bf16[16,128,576]{2,1,0:T(8,128)(2,1)} reshape(bf16[16,73728]{1,0:T(8,128)(2,1)} %fusion.1) | data formatting | bytes 4718592 | tf_op jit(solution)/shard_map/reshape | solution.py:70
  145.7 2.5 %fusion.23 = f32[16,128,128]{1,2,0:T(8,128)S(1)} fusion(bf16[16,128,576]{2,1,0:T(8,128)(2,1)} %reshape.108, bf16[16,128,576]{2,1,0:T(8,128)(2,1)S(1)} %reshape.110, pred[16,128]{1,0:T(8,128)(4,1)S(1)} %iota_compare_fusion.2), kind=kOutput, calls=%fused_computation.26 | convolution fusion | flops 302514176 | bytes 5769216 | tf_op jit(solution)/shard_map/rhc,rtc->rht/dot_general | solution.py:15
  149.4 3.6 %fusion.18 = bf16[16,128,512]{2,1,0:T(8,128)(2,1)} fusion(bf16[16,128,576]{2,1,0:T(8,128)(2,1)S(1)} %reshape.110, f32[16,128]{1,0:T(8,128)S(1)} %fusion.70, f32[16,128,128]{1,2,0:T(8,128)} %copy-done.1), kind=kOutput, calls=%fused_computation.22 | convolution fusion | flops 270272640 | bytes 6299648 | tf_op jit(solution)/shard_map/rht,rtc->rhc/dot_general | solution.py:24
  (64 shorter events, 25.1 us)
Async XLA Ops:
  13.4 25.4 %copy-start.4 = (s32[16]{0:T(128)S(1)}, s32[16]{0:T(128)}, u32[]{:S(2)}) copy-start(s32[16]{0:T(128)} %param.14) | copy-start | bytes 196
  13.4 19.3 %all-to-all-start.2 = ((bf16[4,4,12,1792]{3,1,2,0:T(4,128)(2,1)}), bf16[4,4,12,1792]{3,1,2,0:T(4,128)(2,1)S(1)}, u32[]{:S(2)}, u32[]{:S(2)}) async-start(bf16[4,4,12,1792]{3,1,2,0:T(4,128)(2,1)} %copy.107), calls=%async_computation.2 | async-start | bytes 1376256 | tf_op jit(solution)/shard_map/all_to_all | solution.py:92
  33.9 21.2 %all-to-all-start.3 = ((bf16[4,4,12,1792]{3,0,2,1:T(4,128)(2,1)}), bf16[4,4,12,1792]{3,0,2,1:T(4,128)(2,1)S(1)}, u32[]{:S(2)}, u32[]{:S(2)}) async-start(bf16[4,4,12,1792]{3,0,2,1:T(4,128)(2,1)} %copy.108), calls=%async_computation.3 | async-start | bytes 1376256 | tf_op jit(solution)/shard_map/all_to_all | solution.py:93
  38.8 8.7 %copy-start.6 = (s32[16]{0:T(128)}, s32[16]{0:T(128)S(1)}, u32[]{:S(2)}) copy-start(s32[16]{0:T(128)S(1)} %get-tuple-element.4) | copy-start | bytes 196
  55.1 4.2 %copy-start.2 = (bf16[4,4,12,1792]{3,0,2,1:T(4,128)(2,1)}, bf16[4,4,12,1792]{3,0,2,1:T(4,128)(2,1)S(1)}, u32[]{:S(2)}) copy-start(bf16[4,4,12,1792]{3,0,2,1:T(4,128)(2,1)S(1)} %all-to-all-done.3) | copy-start | bytes 2064388
  55.1 26.8 %all-to-all-start.1 = ((bf16[4,2,36864]{2,1,0:T(2,128)(2,1)}), bf16[4,2,36864]{2,1,0:T(2,128)(2,1)}, u32[]{:S(2)}, u32[]{:S(2)}) async-start(bf16[4,2,36864]{2,1,0:T(2,128)(2,1)} %reshape.118), calls=%async_computation.1 | async-start | bytes 1179648 | tf_op jit(solution)/shard_map/all_to_all | solution.py:61
  59.3 43.5 %all-reduce.3.cloned.1.call-start = ((), (), s32[]{:S(2)}) async-start(), calls=%async_computation.6 | async-start | bytes 1572864 | tf_op jit(solution)/shard_map/psum | solution.py:107
  61.5 4.0 %copy-start.3 = (bf16[192,1792]{1,0:T(8,128)(2,1)S(1)}, bf16[192,1792]{1,0:T(8,128)(2,1)}, u32[]{:S(2)}) copy-start(bf16[192,1792]{1,0:T(8,128)(2,1)} %reshape.112) | copy-start | bytes 2064388
  61.6 4.0 %copy-start.10 = (bf16[1,1792,1024]{2,1,0:T(8,128)(2,1)S(1)}, bf16[1,1792,1024]{2,1,0:T(8,128)(2,1)}, u32[]{:S(2)}) copy-start(bf16[1,1792,1024]{2,1,0:T(8,128)(2,1)} %param.20) | copy-start | bytes 11010052
  71.6 5.4 %copy-start.7 = (s32[16]{0:T(128)S(1)}, s32[16]{0:T(128)}, u32[]{:S(2)}) copy-start(s32[16]{0:T(128)} %copy-done.6) | copy-start | bytes 196
  82.0 27.7 %all-to-all-start = ((bf16[4,2,36864]{2,1,0:T(2,128)(2,1)}), bf16[4,2,36864]{2,1,0:T(2,128)(2,1)}, u32[]{:S(2)}, u32[]{:S(2)}) async-start(bf16[4,2,36864]{2,1,0:T(2,128)(2,1)} %reshape.120), calls=%async_computation | async-start | bytes 1179648 | tf_op jit(solution)/shard_map/all_to_all | solution.py:60
  107.0 8.0 %copy-start.9 = (s32[16]{0:T(128)S(1)}, s32[16]{0:T(128)}, u32[]{:S(2)}) copy-start(s32[16]{0:T(128)} %param.13) | copy-start | bytes 196
  107.0 8.1 %copy-start.8 = (f32[16,2]{0,1:T(2,128)S(1)}, f32[16,2]{0,1:T(2,128)}, u32[]{:S(2)}) copy-start(f32[16,2]{0,1:T(2,128)} %param.18) | copy-start | bytes 388
  109.7 12.6 %copy-start.5 = (s32[16]{0:T(128)S(1)}, s32[16]{0:T(128)}, u32[]{:S(2)}) copy-start(s32[16]{0:T(128)} %param.14) | copy-start | bytes 196
  109.7 16.2 %all-to-all-start.4 = ((bf16[4,4,12,1792]{3,0,2,1:T(4,128)(2,1)}), bf16[4,4,12,1792]{3,0,2,1:T(4,128)(2,1)S(1)}, u32[]{:S(2)}, u32[]{:S(2)}) async-start(bf16[4,4,12,1792]{3,0,2,1:T(4,128)(2,1)} %copy.110), calls=%async_computation.4 | async-start | bytes 1376256 | tf_op jit(solution)/shard_map/all_to_all | solution.py:115
  125.8 6.3 %copy-start = (bf16[16,73728]{1,0:T(8,128)(2,1)S(1)}, bf16[16,73728]{1,0:T(8,128)(2,1)}, u32[]{:S(2)}) copy-start(bf16[16,73728]{1,0:T(8,128)(2,1)} %reshape.107) | copy-start | bytes 7077892
  127.1 26.0 %all-to-all-start.5 = ((bf16[4,4,12,1792]{3,1,2,0:T(4,128)(2,1)}), bf16[4,4,12,1792]{3,1,2,0:T(4,128)(2,1)S(1)}, u32[]{:S(2)}, u32[]{:S(2)}) async-start(bf16[4,4,12,1792]{3,1,2,0:T(4,128)(2,1)} %copy.111), calls=%async_computation.5 | async-start | bytes 1376256 | tf_op jit(solution)/shard_map/all_to_all | solution.py:114
  148.2 1.0 copy-start.1
Sparse Core Ops, SparseCore 0:
  67.4 35.4 all-reduce.2
where the time goes:
time: 164 us; the launch traced here: 162 us
  local copies, waits for them, and re-layouts  51 us (31%)
  waiting for transfers between devices  31.1 us (19%)
  starting transfers between devices  28.6 us (17%)
  matrix products  28.3 us (17%)
  between operations  14.2 us (9%)
  other arithmetic  8.35 us (5%)
    unnamed x29, local copies, waits for them, and re-layouts  21.4 us
    psum x1, waiting for transfers between devices, per_device(): lax.psum(up_part.astype(jnp.bfloat16), 'steal').astype(jnp.float32)  16.5 us
    all_to_all x1, waiting for transfers between devices, per_device(): lax.all_to_all(outgoing, 'ep', split_axis=0, concat_axis=0, tiled=True)  14.5 us
    reshape x1, local copies, waits for them, and re-layouts, per_device(): jnp.where(lent[:, None], taken_queries, query_rows).reshape(queries.shape)  5.46 us
    reshape x1, local copies, waits for them, and re-layouts, per_device(): query_rows = queries.reshape(requests, -1)  5.39 us
    all_to_all x1, starting transfers between devices, per_device(): lax.all_to_all(produced, 'steal', split_axis=1, concat_axis=1, tiled=True)  5.31 us
    all_to_all x1, starting transfers between devices, per_device(): lax.all_to_all(lax.all_to_all(produced, 'steal', split_axis=1, concat_axi...  5.11 us
    all_to_all x1, starting transfers between devices, per_device(): lax.all_to_all(by_expert, 'steal', split_axis=1, concat_axis=1, tiled=True)  4.9 us
  transfers between devices with their start and end apart: 7, of which 2 were waited for; matrix products, arithmetic and copies ran while one was open for 47% of the time, Pallas kernels for 0%

commit v1 on v0

v1 whole, which is shorter than its diff:
```python
import jax
import jax.numpy as jnp
from jax import lax
from jax.experimental import pallas as pl
from jax.experimental.pallas import tpu as pltpu
from jax.sharding import PartitionSpec as P

LAT = 512
CAP_E = 12
CHUNKS = 2

score_scale = 192.0 ** (-0.5)
norm_eps = 1e-06

f32, bf16 = jnp.float32, jnp.bfloat16


def xor_permute(x, axis, m):
    size = lax.axis_size(axis)
    return lax.ppermute(x, axis, [(i, i ^ m) for i in range(size)])


def attention_kernel(index_ref, length_ref, q_ref, c_ref, out_ref):
    i = pl.program_id(0)
    cache = c_ref[0]
    scores = lax.dot_general(
        q_ref[0], cache, (((1,), (1,)), ((), ())), preferred_element_type=f32
    )
    scores = scores * score_scale
    places = lax.broadcasted_iota(jnp.int32, scores.shape, 1)
    scores = jnp.where(places < length_ref[i], scores, -jnp.inf)
    peak = jnp.max(scores, axis=-1, keepdims=True)
    raised = jnp.exp(scores - peak)
    probs = (raised / jnp.sum(raised, axis=-1, keepdims=True)).astype(bf16)
    out_ref[0] = jnp.dot(probs, cache[:, :LAT], preferred_element_type=f32).astype(bf16)


def attend(queries, cache, index, lengths, count, slots, first):
    heads, width = queries.shape[1:]
    positions = cache.shape[1]
    return pl.pallas_call(
        attention_kernel,
        grid_spec=pltpu.PrefetchScalarGridSpec(
            num_scalar_prefetch=2,
            grid=(count,),
            in_specs=[
                pl.BlockSpec((1, heads, width), lambda i, idx, n: (idx[i], 0, 0)),
                pl.BlockSpec((1, positions, width), lambda i, idx, n: (idx[i], 0, 0)),
            ],
            out_specs=pl.BlockSpec((1, heads, LAT), lambda i, idx, n: (first + i, 0, 0)),
        ),
        out_shape=jax.ShapeDtypeStruct((slots, heads, LAT), bf16),
        compiler_params=pltpu.CompilerParams(vmem_limit_bytes=8 * 2**20),
        cost_estimate=pl.CostEstimate(
            flops=2 * count * heads * positions * (width + LAT),
            bytes_accessed=count * 2 * (heads * width + positions * width + heads * LAT),
            transcendentals=count * heads * positions,
        ),
    )(index, lengths, queries, cache)


def place_kernel(where_ref, got_ref, all_ref, out_ref):
    del where_ref, all_ref
    out_ref[...] = got_ref[...]


def per_device(
    queries,
    latent_cache,
    cache_length,
    steal_source,
    hidden,
    norm_gain,
    expert_ids,
    expert_weight,
    w_gate,
    w_up,
    w_down,
):
    s, e = lax.axis_index("steal"), lax.axis_index("ep")
    width, experts = lax.axis_size("steal"), lax.axis_size("ep")
    requests, model_width = hidden.shape
    top = expert_ids.shape[1]
    part = model_width // width
    core = s % 2
    lent = width - 1

    values = hidden.astype(f32)
    scale = lax.rsqrt(jnp.mean(values * values, axis=-1, keepdims=True) + norm_eps)
    normed = (values * scale * norm_gain).astype(bf16)

    high = lax.reduce_precision(expert_weight, 8, 7)
    middle = lax.reduce_precision(expert_weight - high, 8, 7)
    low = expert_weight - high - middle
    meta = jnp.concatenate(
        [cache_length.astype(f32)[:, None], expert_ids.astype(f32), high, middle, low], axis=1
    ).astype(bf16)
    meta = jnp.pad(meta, ((0, 0), (0, 128 - meta.shape[1])))

    rows, metas = [], []
    for m in range(width):
        piece = lax.dynamic_slice(normed, (0, (s ^ m) * part), (requests, part))
        if m == 0:
            rows.append(piece)
            metas.append(meta)
        else:
            got = xor_permute(jnp.concatenate([piece, meta], axis=1), "steal", m)
            rows.append(got[:, :part])
            metas.append(got[:, part:])

    slot_ids = jnp.arange(lent, dtype=jnp.int32)
    offset = (s - steal_source[:lent]) % width
    partner = s ^ ((s + offset) % width)
    peer_lengths = jnp.stack([metas[m][:lent, 0] for m in range(1, width)]).astype(jnp.int32)
    is_partner = partner[None, :] == jnp.arange(1, width, dtype=jnp.int32)[:, None]
    order = jnp.sum(jnp.where(is_partner, slot_ids[None, :], 0), axis=1)
    lent_lengths = jnp.sum(jnp.where(is_partner, peer_lengths, 0), axis=1)
    own = requests - lent
    kept = attend(
        queries,
        latent_cache,
        jnp.arange(lent, requests, dtype=jnp.int32),
        cache_length[lent:],
        own,
        requests,
        lent,
    )
    given = attend(queries, latent_cache, order, lent_lengths, lent, lent, 0)
    taken = jnp.stack([xor_permute(given[m - 1], "steal", m) for m in range(1, width)])
    come_from = s ^ steal_source[:lent]
    where = jnp.sum(
        jnp.where(
            come_from[None, :] == jnp.arange(1, width, dtype=jnp.int32)[:, None],
            slot_ids[None, :],
            0,
        ),
        axis=1,
    )
    heads = queries.shape[1]
    attended = pl.pallas_call(
        place_kernel,
        grid_spec=pltpu.PrefetchScalarGridSpec(
            num_scalar_prefetch=1,
            grid=(lent,),
            in_specs=[
                pl.BlockSpec((1, heads, LAT), lambda i, w: (i, 0, 0)),
                pl.BlockSpec(memory_space=pl.ANY),
            ],
            out_specs=pl.BlockSpec((1, heads, LAT), lambda i, w: (w[i], 0, 0)),
        ),
        out_shape=jax.ShapeDtypeStruct(kept.shape, bf16),
        input_output_aliases={2: 0},
        compiler_params=pltpu.CompilerParams(vmem_limit_bytes=4 * 2**20),
    )(where, taken, kept)

    half = w_gate.shape[2] // 2
    gate_send = lax.dynamic_slice(w_gate[0], (0, (1 - core) * half), (part, half))
    gate_keep = lax.dynamic_slice(w_gate[0], (0, core * half), (part, half))
    up_send = lax.dynamic_slice(w_up[0], (0, (1 - core) * half), (part, half))
    up_keep = lax.dynamic_slice(w_up[0], (0, core * half), (part, half))
    down_own = lax.dynamic_slice(w_down[0], (core * half, 0), (half, part))
    down_other = lax.dynamic_slice(w_down[0], ((1 - core) * half, 0), (half, part))
    tokens = jnp.concatenate(rows, axis=0)
    notes = jnp.concatenate(metas, axis=0).astype(f32)
    ids = notes[:, 1 : 1 + top].astype(jnp.int32)
    weights = (
        notes[:, 1 + top : 1 + 2 * top]
        + notes[:, 1 + 2 * top : 1 + 3 * top]
        + notes[:, 1 + 3 * top : 1 + 4 * top]
    )
    targets = e ^ jnp.arange(experts, dtype=jnp.int32)
    named = ids[:, :, None] == targets[None, None, :]
    hit = jnp.any(named, axis=1)
    share = jnp.sum(jnp.where(named, weights[:, :, None], 0.0), axis=1)
    number = jnp.arange(width * requests, dtype=jnp.int32)
    block = number // requests
    ahead = (block[:, None] == block[None, :]) & (number[None, :] < number[:, None])
    rank = jnp.sum((ahead[:, :, None] & hit[None, :, :]).astype(jnp.int32), axis=1)
    piece = CAP_E // CHUNKS
    room = width * piece
    place = (rank // piece) * room + (s ^ block)[:, None] * piece + rank % piece
    spots = jnp.arange(CHUNKS * room, dtype=jnp.int32).reshape(CHUNKS, 1, room, 1)
    select = hit.T[None, :, None, :] & (place.T[None, :, None, :] == spots)
    weight_map = jnp.where(select, share.T[None, :, None, :], 0.0)
    outgoing = jnp.dot(
        select.reshape(CHUNKS * experts * room, width * requests).astype(bf16),
        tokens,
        preferred_element_type=f32,
    ).astype(bf16)
    outgoing = outgoing.reshape(CHUNKS, experts, room, part)

    mixed = jnp.zeros((width * requests, part), f32)
    for chunk in range(CHUNKS):
        arrived = jnp.concatenate(
            [outgoing[chunk, 0]]
            + [xor_permute(outgoing[chunk, n], "ep", n) for n in range(1, experts)],
            axis=0,
        )
        send = jnp.concatenate(
            [
                jnp.dot(arrived, gate_send, preferred_element_type=f32).astype(bf16),
                jnp.dot(arrived, up_send, preferred_element_type=f32).astype(bf16),
            ],
            axis=1,
        )
        got = xor_permute(send, "steal", 1)
        keep = jnp.concatenate(
            [
                jnp.dot(arrived, gate_keep, preferred_element_type=f32),
                jnp.dot(arrived, up_keep, preferred_element_type=f32),
            ],
            axis=1,
        )
        total = (keep + got.astype(f32)).astype(bf16)
        step = 2
        while step < width:
            total = (total.astype(f32) + xor_permute(total, "steal", step).astype(f32)).astype(bf16)
            step *= 2
        total = total.astype(f32)
        active = (jax.nn.silu(total[:, :half]) * total[:, half:]).astype(bf16)
        other = xor_permute(active, "steal", 1)
        produced = (
            jnp.dot(active, down_own, preferred_element_type=f32)
            + jnp.dot(other, down_other, preferred_element_type=f32)
        ).astype(bf16)
        produced = produced.reshape(experts, room, part)
        returned = jnp.concatenate(
            [produced[0]] + [xor_permute(produced[n], "ep", n) for n in range(1, experts)],
            axis=0,
        )
        mixed = mixed + jnp.einsum(
            "ir,ik->rk",
            weight_map[chunk].reshape(experts * room, width * requests),
            returned.astype(f32),
            precision=lax.Precision.HIGHEST,
            preferred_element_type=f32,
        )
    mixed = mixed.astype(bf16).reshape(width, requests, part)
    result = jnp.zeros((requests, model_width), bf16)
    for m in range(width):
        got = mixed[m] if m == 0 else xor_permute(mixed[m], "steal", m)
        result = lax.dynamic_update_slice(result, got, (0, (s ^ m) * part))
    return (attended, result)


def solution(mesh):
    return jax.shard_map(
        per_device,
        mesh=mesh,
        in_specs=(
            P(("rep", "steal", "ep"), None, None),
            P(("rep", "steal", "ep"), None, None),
            P(("rep", "steal", "ep")),
            P(("rep", "steal", "ep")),
            P(("rep", "steal", "ep"), None),
            P(),
            P(("rep", "steal", "ep"), None),
            P(("rep", "steal", "ep"), None),
            P("ep", "steal", None),
            P("ep", "steal", None),
            P("ep", None, "steal"),
        ),
        out_specs=(P(("rep", "steal", "ep"), None, None), P(("rep", "steal", "ep"), None)),
        check_vma=False,
    )
```

time: 164 us -> 105 us (0.64)
  local copies, waits for them, and re-layouts: 51 us -> 19.9 us
  matrix products: 28.3 us -> 6.86 us
  Pallas kernels: 0 us -> 13.3 us
  between operations: 14.2 us -> 1.12 us
  waiting for transfers between devices: 31.1 us -> 20 us
  starting transfers between devices: 28.6 us -> 34.3 us
    ppermute x0 -> x27, starting transfers between devices: none -> 34.3 us  [xor_permute(): return lax.ppermute(x, axis, [(i, i ^ m) for i in range(size)])]
    all_to_all x6 -> x0, starting transfers between devices: 28.6 us -> none  [the longest x1 5.31 us: per_device(): lax.all_to_all(produced, 'steal', split_axis=1, concat_axis=1, tiled=True)]
    reshape x8 -> x0, local copies, waits for them, and re-layouts: 23.4 us -> none  [the longest x1 5.46 us: per_device(): jnp.where(lent[:, None], taken_queries, query_rows).reshape(queries.shape)]
    dot_general x11 -> x15, matrix products: 28.3 us -> 6.86 us  [the longest x2 0.89 us: per_device(): jnp.dot(arrived, up_send, preferred_element_type=f32).astype(bf16)]
    ppermute x0 -> x27, waiting for transfers between devices: none -> 20 us  [xor_permute(): return lax.ppermute(x, axis, [(i, i ^ m) for i in range(size)])]
    psum x1 -> x0, waiting for transfers between devices: 16.5 us -> none  [per_device(): lax.psum(up_part.astype(jnp.bfloat16), 'steal').astype(jnp.float32)]
    all_to_all x6 -> x0, waiting for transfers between devices: 14.5 us -> none  [the longest x1 14.5 us: per_device(): lax.all_to_all(outgoing, 'ep', split_axis=0, concat_axis=0, tiled=True)]
    pallas_call x0 -> x3, Pallas kernels: none -> 13.3 us  [the longest x2 11.4 us: attend(): pl.pallas_call(attention_kernel, grid_spec=pltpu.PrefetchScalarGridSpec(n...]
  transfers between devices with their start and end apart: 7 -> 27, of which waited for: 2 -> 7; matrix products, arithmetic and copies ran while one was open for 47% -> 17% of each run, Pallas kernels for 0% -> 13%
where the time goes in v1:
time: 105 us; the launch traced here: 104 us
  starting transfers between devices  34.3 us (33%)
  waiting for transfers between devices  20 us (19%)
  local copies, waits for them, and re-layouts  19.9 us (19%)
  Pallas kernels  13.3 us (13%)
  other arithmetic  8.61 us (8%)
  matrix products  6.86 us (7%)
  between operations  1.12 us (1%)
    ppermute x27, starting transfers between devices, xor_permute(): return lax.ppermute(x, axis, [(i, i ^ m) for i in range(size)])  34.3 us
    ppermute x27, waiting for transfers between devices, xor_permute(): return lax.ppermute(x, axis, [(i, i ^ m) for i in range(size)])  20 us
    unnamed x21, local copies, waits for them, and re-layouts  11.7 us
    pallas_call x2, Pallas kernels, attend(): pl.pallas_call(attention_kernel, grid_spec=pltpu.PrefetchScalarGridSpec(n...  11.4 us
    slice x3, local copies, waits for them, and re-layouts, per_device(): rows.append(got[:, :part])  3.3 us
    convert_element_type x1, other arithmetic, per_device(): normed = (values * scale * norm_gain).astype(bf16)  3 us
    slice x3, local copies, waits for them, and re-layouts, per_device(): metas.append(got[:, part:])  2.28 us
  transfers between devices with their start and end apart: 27, of which 7 were waited for; matrix products, arithmetic and copies ran while one was open for 17% of the time, Pallas kernels for 13%

profile of v1, /device:TPU:17, one launch (start us, length us, event | category | flops | bytes accessed | tf_op | source)
XLA Modules:
  0.0 104.1 jit_solution(14107988608699957616)
XLA Ops:
  2.7 1.8 %copy.64 = bf16[16,7168]{0,1:T(8,128)(2,1)S(1)} copy(bf16[16,7168]{1,0:T(8,128)(2,1)} %param.15) | data formatting | bytes 458752 | tf_op args[4]
  5.6 3.0 %fusion.2 = bf16[16,7168]{0,1:T(8,128)(2,1)S(1)} fusion(bf16[16,7168]{0,1:T(8,128)(2,1)S(1)} %copy.64, f32[7168]{0:T(1024)S(1)} %copy-done.4, f32[16]{0:T(128)S(1)} %add_rsqrt_fusion), kind=kLoop, calls=%fused_computation.4 | loop fusion | flops 458752 | bytes 487488 | tf_op jit(solution)/shard_map/convert_element_type | solution.py:90
  12.7 3.1 %copy.65.q_ref = bf16[16,128,576]{2,1,0:T(8,128)(2,1)S(1)} copy(bf16[16,128,576]{1,2,0:T(8,128)(2,1)} %param.11) | data formatting | bytes 4718592 | tf_op args[0]
  15.8 4.4 %copy.66.c_ref = bf16[16,128,576]{2,1,0:T(8,128)(2,1)} copy(bf16[16,128,576]{1,2,0:T(8,128)(2,1)} %param.12) | data formatting | bytes 4718592 | tf_op args[1]
  20.1 1.7 %copy-done = bf16[16,128,576]{2,1,0:T(8,128)(2,1)S(1)} copy-done((bf16[16,128,576]{2,1,0:T(8,128)(2,1)S(1)}, bf16[16,128,576]{2,1,0:T(8,128)(2,1)}, u32[]{:S(2)}) %copy-start) | copy-done | bytes 2359320
  21.8 9.0 %shard_map.123.all_ref = bf16[16,128,512]{2,1,0:T(8,128)(2,1)} custom-call(s32[13]{0:T(128)S(1)} %iota_add_fusion.index_ref, s32[13]{0:T(128)S(1)} %slice.155.length_ref, bf16[16,128,576]{2,1,0:T(8,128)(2,1)S(1)} %copy.65.q_ref, bf16[16,128,576]{2,1,0:T(8,128)(2,1)S(1)} %copy-done), custom_call_target="tpu_custom_call" | custom-call | flops 463470592 | bytes 5537792 | tf_op jit(solution)/shard_map/pallas_call | solution.py:41
  32.3 2.1 %collective-permute-done.2 = bf16[16,1920]{0,1:T(8,128)(2,1)} collective-permute-done((bf16[16,1920]{0,1:T(8,128)(2,1)}, bf16[16,1920]{0,1:T(8,128)(2,1)}, u32[]{:S(2)}, u32[]{:S(2)}) %collective-permute-start.2) | collective-permute-done | bytes 61472 | tf_op jit(solution)/shard_map/ppermute | solution.py:20
  40.3 3.2 %collective-permute-start.16 = (bf16[24,1792]{1,0:T(8,128)(2,1)S(1)}, bf16[24,1792]{1,0:T(8,128)(2,1)S(1)}, u32[]{:S(2)}, u32[]{:S(2)}) collective-permute-start(bf16[24,1792]{1,0:T(8,128)(2,1)S(1)} %get-tuple-element.11), channel_id=1, source_target_pairs={{0,2},{1,3},{2,0},{3,1},{4,6},{5,7},{6,4},{7,5},{8,10},{9,11},{10,... | collective-permute-start | bytes 258056 | tf_op jit(solution)/shard_map/ppermute | solution.py:20
  45.8 2.4 %shard_map.122 = bf16[3,128,512]{2,1,0:T(8,128)(2,1)S(1)} custom-call(s32[3]{0:T(128)S(1)} %get-tuple-element.3.index_ref, s32[3]{0:T(128)S(1)} %get-tuple-element.2.length_ref, bf16[16,128,576]{2,1,0:T(8,128)(2,1)S(1)} %copy.65.q_ref, bf16[16,128,576]{2,1,0:T(8,128)(2,1)S(1)} %copy-done.1), custom_call_target="tpu_custom_call" | custom-call | flops 106954752 | bytes 1277952 | tf_op jit(solution)/shard_map/pallas_call | solution.py:41
  48.6 3.3 %collective-permute-start.7 = (bf16[24,1792]{1,0:T(8,128)(2,1)S(1)}, bf16[24,1792]{1,0:T(8,128)(2,1)S(1)}, u32[]{:S(2)}, u32[]{:S(2)}) collective-permute-start(bf16[24,1792]{1,0:T(8,128)(2,1)S(1)} %get-tuple-element.15), channel_id=1, source_target_pairs={{0,2},{1,3},{2,0},{3,1},{4,6},{5,7},{6,4},{7,5},{8,10},{9,11},{10,... | collective-permute-start | bytes 258056 | tf_op jit(solution)/shard_map/ppermute | solution.py:20
  51.9 1.8 %collective-permute-start.3 = (bf16[128,512]{1,0:T(8,128)(2,1)S(1)}, bf16[128,512]{1,0:T(8,128)(2,1)S(1)}, u32[]{:S(2)}, u32[]{:S(2)}) collective-permute-start(bf16[128,512]{1,0:T(8,128)(2,1)S(1)} %get-tuple-element.17), channel_id=1, source_target_pairs={{0,4},{4,0},{8,12},{12,8},{1,5},{5,1},{9,13},{13,9},{2,6},{6,2},{1... | collective-permute-start | bytes 393224 | tf_op jit(solution)/shard_map/ppermute | solution.py:20
  55.7 2.4 %collective-permute-start.18 = (bf16[96,1024]{1,0:T(8,128)(2,1)S(1)}, bf16[96,1024]{1,0:T(8,128)(2,1)S(1)}, u32[]{:S(2)}, u32[]{:S(2)}) collective-permute-start(bf16[96,1024]{1,0:T(8,128)(2,1)S(1)} %pad_maximum_fusion.7), channel_id=1, source_target_pairs={{0,4},{4,0},{8,12},{12,8},{1,5},{5,1},{9,13},{13,9},{2,6},{6,2},{1... | collective-permute-start | bytes 589832 | tf_op jit(solution)/shard_map/ppermute | solution.py:20
  62.7 4.4 %collective-permute-done.19 = bf16[96,1024]{1,0:T(8,128)(2,1)S(1)} collective-permute-done((bf16[96,1024]{1,0:T(8,128)(2,1)S(1)}, bf16[96,1024]{1,0:T(8,128)(2,1)S(1)}, u32[]{:S(2)}, u32[]{:S(2)}) %collective-permute-start.19) | collective-permute-done | bytes 196640 | tf_op jit(solution)/shard_map/ppermute | solution.py:20
  67.2 2.3 %collective-permute-start.20 = (bf16[96,512]{1,0:T(8,128)(2,1)S(1)}, bf16[96,512]{1,0:T(8,128)(2,1)S(1)}, u32[]{:S(2)}, u32[]{:S(2)}) collective-permute-start(bf16[96,512]{1,0:T(8,128)(2,1)S(1)} %fusion.78), channel_id=1, source_target_pairs={{0,4},{4,0},{8,12},{12,8},{1,5},{5,1},{9,13},{13,9},{2,6},{6,2},{1... | collective-permute-start | bytes 294920 | tf_op jit(solution)/shard_map/ppermute | solution.py:20
  69.6 1.8 %collective-permute-done.10 = bf16[96,1024]{1,0:T(8,128)(2,1)S(1)} collective-permute-done((bf16[96,1024]{1,0:T(8,128)(2,1)S(1)}, bf16[96,1024]{1,0:T(8,128)(2,1)S(1)}, u32[]{:S(2)}, u32[]{:S(2)}) %collective-permute-start.10) | collective-permute-done | bytes 196640 | tf_op jit(solution)/shard_map/ppermute | solution.py:20
  71.4 1.4 %collective-permute-start.11 = (bf16[96,512]{1,0:T(8,128)(2,1)S(1)}, bf16[96,512]{1,0:T(8,128)(2,1)S(1)}, u32[]{:S(2)}, u32[]{:S(2)}) collective-permute-start(bf16[96,512]{1,0:T(8,128)(2,1)S(1)} %fusion.79), channel_id=1, source_target_pairs={{0,4},{4,0},{8,12},{12,8},{1,5},{5,1},{9,13},{13,9},{2,6},{6,2},{1... | collective-permute-start | bytes 294920 | tf_op jit(solution)/shard_map/ppermute | solution.py:20
  75.4 3.0 %collective-permute-start.22 = (bf16[24,1792]{1,0:T(8,128)(2,1)S(1)}, bf16[24,1792]{1,0:T(8,128)(2,1)S(1)}, u32[]{:S(2)}, u32[]{:S(2)}) collective-permute-start(bf16[24,1792]{1,0:T(8,128)(2,1)S(1)} %get-tuple-element.26), channel_id=1, source_target_pairs={{0,2},{1,3},{2,0},{3,1},{4,6},{5,7},{6,4},{7,5},{8,10},{9,11},{10,... | collective-permute-start | bytes 258056 | tf_op jit(solution)/shard_map/ppermute | solution.py:20
  79.5 3.6 %collective-permute-done.22 = bf16[24,1792]{1,0:T(8,128)(2,1)S(1)} collective-permute-done((bf16[24,1792]{1,0:T(8,128)(2,1)S(1)}, bf16[24,1792]{1,0:T(8,128)(2,1)S(1)}, u32[]{:S(2)}, u32[]{:S(2)}) %collective-permute-start.22) | collective-permute-done | bytes 86048 | tf_op jit(solution)/shard_map/ppermute | solution.py:20
  83.2 3.1 %collective-permute-start.13 = (bf16[24,1792]{1,0:T(8,128)(2,1)S(1)}, bf16[24,1792]{1,0:T(8,128)(2,1)S(1)}, u32[]{:S(2)}, u32[]{:S(2)}) collective-permute-start(bf16[24,1792]{1,0:T(8,128)(2,1)S(1)} %get-tuple-element.22), channel_id=1, source_target_pairs={{0,2},{1,3},{2,0},{3,1},{4,6},{5,7},{6,4},{7,5},{8,10},{9,11},{10,... | collective-permute-start | bytes 258056 | tf_op jit(solution)/shard_map/ppermute | solution.py:20
  86.7 3.7 %collective-permute-done.14 = bf16[24,1792]{1,0:T(8,128)(2,1)S(1)} collective-permute-done((bf16[24,1792]{1,0:T(8,128)(2,1)S(1)}, bf16[24,1792]{1,0:T(8,128)(2,1)S(1)}, u32[]{:S(2)}, u32[]{:S(2)}) %collective-permute-start.14) | collective-permute-done | bytes 86048 | tf_op jit(solution)/shard_map/ppermute | solution.py:20
  92.0 1.5 %collective-permute-start.24 = (bf16[16,1792]{1,0:T(8,128)(2,1)S(1)}, bf16[16,1792]{1,0:T(8,128)(2,1)S(1)}, u32[]{:S(2)}, u32[]{:S(2)}) collective-permute-start(bf16[16,1792]{1,0:T(8,128)(2,1)S(1)} %get-tuple-element.30), channel_id=1, source_target_pairs={{0,4},{4,0},{8,12},{12,8},{1,5},{5,1},{9,13},{13,9},{2,6},{6,2},{1... | collective-permute-start | bytes 172040 | tf_op jit(solution)/shard_map/ppermute | solution.py:20
  94.3 1.9 %shard_map.124 = bf16[16,128,512]{2,1,0:T(8,128)(2,1)} custom-call(s32[3]{0:T(128)S(1)} %get-tuple-element.4.where_ref, bf16[3,128,512]{2,1,0:T(8,128)(2,1)S(1)} %pad_maximum_fusion.3.got_ref, bf16[16,128,512]{2,1,0:T(8,128)(2,1)} %shard_map.123.all_ref), custom_call_target="tpu_custom_call", output_to_operand_aliasing={{}: (2, {})} | custom-call | tf_op jit(solution)/shard_map/pallas_call | solution.py:140
  96.2 3.3 %collective-permute-start.26 = (bf16[16,1792]{1,0:T(8,128)(2,1)S(1)}, bf16[16,1792]{1,0:T(8,128)(2,1)S(1)}, u32[]{:S(2)}, u32[]{:S(2)}) collective-permute-start(bf16[16,1792]{1,0:T(8,128)(2,1)S(1)} %get-tuple-element.28), channel_id=1, source_target_pairs={{0,12},{4,8},{8,4},{12,0},{1,13},{5,9},{9,5},{13,1},{2,14},{6,10},... | collective-permute-start | bytes 172040 | tf_op jit(solution)/shard_map/ppermute | solution.py:20
  99.7 3.6 %collective-permute-done.25 = bf16[16,1792]{1,0:T(8,128)(2,1)S(1)} collective-permute-done((bf16[16,1792]{1,0:T(8,128)(2,1)S(1)}, bf16[16,1792]{1,0:T(8,128)(2,1)S(1)}, u32[]{:S(2)}, u32[]{:S(2)}) %collective-permute-start.25) | collective-permute-done | bytes 57376 | tf_op jit(solution)/shard_map/ppermute | solution.py:20
  (126 shorter events, 31.1 us)
Async XLA Ops:
  10.0 20.8 %collective-permute-start = (bf16[16,1920]{0,1:T(8,128)(2,1)}, bf16[16,1920]{0,1:T(8,128)(2,1)}, u32[]{:S(2)}, u32[]{:S(2)}) collective-permute-start(bf16[16,1920]{0,1:T(8,128)(2,1)} %get-tuple-element.34), channel_id=1, source_target_pairs={{0,4},{4,0},{8,12},{12,8},{1,5},{5,1},{9,13},{13,9},{2,6},{6,2},{1... | collective-permute-start | bytes 184328 | tf_op jit(solution)/shard_map/ppermute | solution.py:20
  10.7 20.9 %collective-permute-start.1 = (bf16[16,1920]{0,1:T(8,128)(2,1)}, bf16[16,1920]{0,1:T(8,128)(2,1)}, u32[]{:S(2)}, u32[]{:S(2)}) collective-permute-start(bf16[16,1920]{0,1:T(8,128)(2,1)} %get-tuple-element.35), channel_id=1, source_target_pairs={{0,8},{4,12},{8,0},{12,4},{1,9},{5,13},{9,1},{13,5},{2,10},{6,14},... | collective-permute-start | bytes 184328 | tf_op jit(solution)/shard_map/ppermute | solution.py:20
  11.9 22.6 %collective-permute-start.2 = (bf16[16,1920]{0,1:T(8,128)(2,1)}, bf16[16,1920]{0,1:T(8,128)(2,1)}, u32[]{:S(2)}, u32[]{:S(2)}) collective-permute-start(bf16[16,1920]{0,1:T(8,128)(2,1)} %get-tuple-element.36), channel_id=1, source_target_pairs={{0,12},{4,8},{8,4},{12,0},{1,13},{5,9},{9,5},{13,1},{2,14},{6,10},... | collective-permute-start | bytes 184328 | tf_op jit(solution)/shard_map/ppermute | solution.py:20
  40.1 11.8 %collective-permute-start.17 = (bf16[24,1792]{1,0:T(8,128)(2,1)S(1)}, bf16[24,1792]{1,0:T(8,128)(2,1)S(1)}, u32[]{:S(2)}, u32[]{:S(2)}) collective-permute-start(bf16[24,1792]{1,0:T(8,128)(2,1)S(1)} %get-tuple-element.10), channel_id=1, source_target_pairs={{0,3},{1,2},{2,1},{3,0},{4,7},{5,6},{6,5},{7,4},{8,11},{9,10},{10,... | collective-permute-start | bytes 258056 | tf_op jit(solution)/shard_map/ppermute | solution.py:20
  40.3 11.5 %collective-permute-start.16 = (bf16[24,1792]{1,0:T(8,128)(2,1)S(1)}, bf16[24,1792]{1,0:T(8,128)(2,1)S(1)}, u32[]{:S(2)}, u32[]{:S(2)}) collective-permute-start(bf16[24,1792]{1,0:T(8,128)(2,1)S(1)} %get-tuple-element.11), channel_id=1, source_target_pairs={{0,2},{1,3},{2,0},{3,1},{4,6},{5,7},{6,4},{7,5},{8,10},{9,11},{10,... | collective-permute-start | bytes 258056 | tf_op jit(solution)/shard_map/ppermute | solution.py:20
  43.5 10.1 %collective-permute-start.15 = (bf16[24,1792]{1,0:T(8,128)(2,1)S(1)}, bf16[24,1792]{1,0:T(8,128)(2,1)S(1)}, u32[]{:S(2)}, u32[]{:S(2)}) collective-permute-start(bf16[24,1792]{1,0:T(8,128)(2,1)S(1)} %get-tuple-element.12), channel_id=1, source_target_pairs={{0,1},{1,0},{2,3},{3,2},{4,5},{5,4},{6,7},{7,6},{8,9},{9,8},{10,11... | collective-permute-start | bytes 258056 | tf_op jit(solution)/shard_map/ppermute | solution.py:20
  48.2 7.5 %collective-permute-start.8 = (bf16[24,1792]{1,0:T(8,128)(2,1)S(1)}, bf16[24,1792]{1,0:T(8,128)(2,1)S(1)}, u32[]{:S(2)}, u32[]{:S(2)}) collective-permute-start(bf16[24,1792]{1,0:T(8,128)(2,1)S(1)} %get-tuple-element.14), channel_id=1, source_target_pairs={{0,3},{1,2},{2,1},{3,0},{4,7},{5,6},{6,5},{7,4},{8,11},{9,10},{10,... | collective-permute-start | bytes 258056 | tf_op jit(solution)/shard_map/ppermute | solution.py:20
  48.6 9.6 %collective-permute-start.7 = (bf16[24,1792]{1,0:T(8,128)(2,1)S(1)}, bf16[24,1792]{1,0:T(8,128)(2,1)S(1)}, u32[]{:S(2)}, u32[]{:S(2)}) collective-permute-start(bf16[24,1792]{1,0:T(8,128)(2,1)S(1)} %get-tuple-element.15), channel_id=1, source_target_pairs={{0,2},{1,3},{2,0},{3,1},{4,6},{5,7},{6,4},{7,5},{8,10},{9,11},{10,... | collective-permute-start | bytes 258056 | tf_op jit(solution)/shard_map/ppermute | solution.py:20
  51.9 6.3 %collective-permute-start.6 = (bf16[24,1792]{1,0:T(8,128)(2,1)S(1)}, bf16[24,1792]{1,0:T(8,128)(2,1)S(1)}, u32[]{:S(2)}, u32[]{:S(2)}) collective-permute-start(bf16[24,1792]{1,0:T(8,128)(2,1)S(1)} %get-tuple-element.16), channel_id=1, source_target_pairs={{0,1},{1,0},{2,3},{3,2},{4,5},{5,4},{6,7},{7,6},{8,9},{9,8},{10,11... | collective-permute-start | bytes 258056 | tf_op jit(solution)/shard_map/ppermute | solution.py:20
  51.9 41.6 %collective-permute-start.3 = (bf16[128,512]{1,0:T(8,128)(2,1)S(1)}, bf16[128,512]{1,0:T(8,128)(2,1)S(1)}, u32[]{:S(2)}, u32[]{:S(2)}) collective-permute-start(bf16[128,512]{1,0:T(8,128)(2,1)S(1)} %get-tuple-element.17), channel_id=1, source_target_pairs={{0,4},{4,0},{8,12},{12,8},{1,5},{5,1},{9,13},{13,9},{2,6},{6,2},{1... | collective-permute-start | bytes 393224 | tf_op jit(solution)/shard_map/ppermute | solution.py:20
  53.6 39.9 %collective-permute-start.5 = (bf16[128,512]{1,0:T(8,128)(2,1)S(1)}, bf16[128,512]{1,0:T(8,128)(2,1)S(1)}, u32[]{:S(2)}, u32[]{:S(2)}) collective-permute-start(bf16[128,512]{1,0:T(8,128)(2,1)S(1)} %get-tuple-element.18), channel_id=1, source_target_pairs={{0,12},{4,8},{8,4},{12,0},{1,13},{5,9},{9,5},{13,1},{2,14},{6,10},... | collective-permute-start | bytes 393224 | tf_op jit(solution)/shard_map/ppermute | solution.py:20
  55.7 5.3 %collective-permute-start.18 = (bf16[96,1024]{1,0:T(8,128)(2,1)S(1)}, bf16[96,1024]{1,0:T(8,128)(2,1)S(1)}, u32[]{:S(2)}, u32[]{:S(2)}) collective-permute-start(bf16[96,1024]{1,0:T(8,128)(2,1)S(1)} %pad_maximum_fusion.7), channel_id=1, source_target_pairs={{0,4},{4,0},{8,12},{12,8},{1,5},{5,1},{9,13},{13,9},{2,6},{6,2},{1... | collective-permute-start | bytes 589832 | tf_op jit(solution)/shard_map/ppermute | solution.py:20
  61.1 6.1 %collective-permute-start.19 = (bf16[96,1024]{1,0:T(8,128)(2,1)S(1)}, bf16[96,1024]{1,0:T(8,128)(2,1)S(1)}, u32[]{:S(2)}, u32[]{:S(2)}) collective-permute-start(bf16[96,1024]{1,0:T(8,128)(2,1)S(1)} %fusion.60), channel_id=1, source_target_pairs={{0,8},{4,12},{8,0},{12,4},{1,9},{5,13},{9,1},{13,5},{2,10},{6,14},... | collective-permute-start | bytes 589832 | tf_op jit(solution)/shard_map/ppermute | solution.py:20
  62.4 8.9 %collective-permute-start.10 = (bf16[96,1024]{1,0:T(8,128)(2,1)S(1)}, bf16[96,1024]{1,0:T(8,128)(2,1)S(1)}, u32[]{:S(2)}, u32[]{:S(2)}) collective-permute-start(bf16[96,1024]{1,0:T(8,128)(2,1)S(1)} %fusion.59), channel_id=1, source_target_pairs={{0,8},{4,12},{8,0},{12,4},{1,9},{5,13},{9,1},{13,5},{2,10},{6,14},... | collective-permute-start | bytes 589832 | tf_op jit(solution)/shard_map/ppermute | solution.py:20
  67.2 6.5 %collective-permute-start.20 = (bf16[96,512]{1,0:T(8,128)(2,1)S(1)}, bf16[96,512]{1,0:T(8,128)(2,1)S(1)}, u32[]{:S(2)}, u32[]{:S(2)}) collective-permute-start(bf16[96,512]{1,0:T(8,128)(2,1)S(1)} %fusion.78), channel_id=1, source_target_pairs={{0,4},{4,0},{8,12},{12,8},{1,5},{5,1},{9,13},{13,9},{2,6},{6,2},{1... | collective-permute-start | bytes 294920 | tf_op jit(solution)/shard_map/ppermute | solution.py:20
  71.4 7.0 %collective-permute-start.11 = (bf16[96,512]{1,0:T(8,128)(2,1)S(1)}, bf16[96,512]{1,0:T(8,128)(2,1)S(1)}, u32[]{:S(2)}, u32[]{:S(2)}) collective-permute-start(bf16[96,512]{1,0:T(8,128)(2,1)S(1)} %fusion.79), channel_id=1, source_target_pairs={{0,4},{4,0},{8,12},{12,8},{1,5},{5,1},{9,13},{13,9},{2,6},{6,2},{1... | collective-permute-start | bytes 294920 | tf_op jit(solution)/shard_map/ppermute | solution.py:20
  74.2 4.7 %collective-permute-start.23 = (bf16[24,1792]{1,0:T(8,128)(2,1)S(1)}, bf16[24,1792]{1,0:T(8,128)(2,1)S(1)}, u32[]{:S(2)}, u32[]{:S(2)}) collective-permute-start(bf16[24,1792]{1,0:T(8,128)(2,1)S(1)} %get-tuple-element.25), channel_id=1, source_target_pairs={{0,3},{1,2},{2,1},{3,0},{4,7},{5,6},{6,5},{7,4},{8,11},{9,10},{10,... | collective-permute-start | bytes 258056 | tf_op jit(solution)/shard_map/ppermute | solution.py:20
  75.4 7.8 %collective-permute-start.22 = (bf16[24,1792]{1,0:T(8,128)(2,1)S(1)}, bf16[24,1792]{1,0:T(8,128)(2,1)S(1)}, u32[]{:S(2)}, u32[]{:S(2)}) collective-permute-start(bf16[24,1792]{1,0:T(8,128)(2,1)S(1)} %get-tuple-element.26), channel_id=1, source_target_pairs={{0,2},{1,3},{2,0},{3,1},{4,6},{5,7},{6,4},{7,5},{8,10},{9,11},{10,... | collective-permute-start | bytes 258056 | tf_op jit(solution)/shard_map/ppermute | solution.py:20
  78.4 7.8 %collective-permute-start.21 = (bf16[24,1792]{1,0:T(8,128)(2,1)S(1)}, bf16[24,1792]{1,0:T(8,128)(2,1)S(1)}, u32[]{:S(2)}, u32[]{:S(2)}) collective-permute-start(bf16[24,1792]{1,0:T(8,128)(2,1)S(1)} %get-tuple-element.27), channel_id=1, source_target_pairs={{0,1},{1,0},{2,3},{3,2},{4,5},{5,4},{6,7},{7,6},{8,9},{9,8},{10,11... | collective-permute-start | bytes 258056 | tf_op jit(solution)/shard_map/ppermute | solution.py:20
  78.9 11.5 %collective-permute-start.14 = (bf16[24,1792]{1,0:T(8,128)(2,1)S(1)}, bf16[24,1792]{1,0:T(8,128)(2,1)S(1)}, u32[]{:S(2)}, u32[]{:S(2)}) collective-permute-start(bf16[24,1792]{1,0:T(8,128)(2,1)S(1)} %get-tuple-element.21), channel_id=1, source_target_pairs={{0,3},{1,2},{2,1},{3,0},{4,7},{5,6},{6,5},{7,4},{8,11},{9,10},{10,... | collective-permute-start | bytes 258056 | tf_op jit(solution)/shard_map/ppermute | solution.py:20
  83.2 8.4 %collective-permute-start.13 = (bf16[24,1792]{1,0:T(8,128)(2,1)S(1)}, bf16[24,1792]{1,0:T(8,128)(2,1)S(1)}, u32[]{:S(2)}, u32[]{:S(2)}) collective-permute-start(bf16[24,1792]{1,0:T(8,128)(2,1)S(1)} %get-tuple-element.22), channel_id=1, source_target_pairs={{0,2},{1,3},{2,0},{3,1},{4,6},{5,7},{6,4},{7,5},{8,10},{9,11},{10,... | collective-permute-start | bytes 258056 | tf_op jit(solution)/shard_map/ppermute | solution.py:20
  86.3 5.3 %collective-permute-start.12 = (bf16[24,1792]{1,0:T(8,128)(2,1)S(1)}, bf16[24,1792]{1,0:T(8,128)(2,1)S(1)}, u32[]{:S(2)}, u32[]{:S(2)}) collective-permute-start(bf16[24,1792]{1,0:T(8,128)(2,1)S(1)} %get-tuple-element.23), channel_id=1, source_target_pairs={{0,1},{1,0},{2,3},{3,2},{4,5},{5,4},{6,7},{7,6},{8,9},{9,8},{10,11... | collective-permute-start | bytes 258056 | tf_op jit(solution)/shard_map/ppermute | solution.py:20
  92.0 7.7 %collective-permute-start.24 = (bf16[16,1792]{1,0:T(8,128)(2,1)S(1)}, bf16[16,1792]{1,0:T(8,128)(2,1)S(1)}, u32[]{:S(2)}, u32[]{:S(2)}) collective-permute-start(bf16[16,1792]{1,0:T(8,128)(2,1)S(1)} %get-tuple-element.30), channel_id=1, source_target_pairs={{0,4},{4,0},{8,12},{12,8},{1,5},{5,1},{9,13},{13,9},{2,6},{6,2},{1... | collective-permute-start | bytes 172040 | tf_op jit(solution)/shard_map/ppermute | solution.py:20
  96.2 7.2 %collective-permute-start.26 = (bf16[16,1792]{1,0:T(8,128)(2,1)S(1)}, bf16[16,1792]{1,0:T(8,128)(2,1)S(1)}, u32[]{:S(2)}, u32[]{:S(2)}) collective-permute-start(bf16[16,1792]{1,0:T(8,128)(2,1)S(1)} %get-tuple-element.28), channel_id=1, source_target_pairs={{0,12},{4,8},{8,4},{12,0},{1,13},{5,9},{9,5},{13,1},{2,14},{6,10},... | collective-permute-start | bytes 172040 | tf_op jit(solution)/shard_map/ppermute | solution.py:20
  (12 other events, 61.7 us)

commit v2 on v1

v2 whole, which is shorter than its diff:
```python
import functools

import jax
import jax.numpy as jnp
from jax import lax
from jax.experimental import pallas as pl
from jax.experimental.pallas import tpu as pltpu
from jax.sharding import PartitionSpec as P

LAT = 512
CAP_E = 12
CHUNKS = 2
LANES = 128
ATTEND_VMEM = 12 * 2**20
NOTES = 16

score_scale = 192.0 ** (-0.5)
norm_eps = 1e-06

f32, bf16 = jnp.float32, jnp.bfloat16
vmem = pl.BlockSpec(memory_space=pltpu.VMEM)
hbm = pl.BlockSpec(memory_space=pltpu.HBM)
smem = pl.BlockSpec(memory_space=pltpu.SMEM)


def xor_permute(x, axis, m):
    size = lax.axis_size(axis)
    return lax.ppermute(x, axis, [(i, i ^ m) for i in range(size)])


def prepare_kernel(
    width, here_ref, hidden_ref, gain_ref, length_ref, ids_ref, weight_ref, *refs
):
    messages, (normed_ref, notes_ref) = refs[:width], refs[width:]
    s = here_ref[0]
    requests, model_width = hidden_ref.shape
    part = model_width // width
    top = ids_ref.shape[0]
    values = hidden_ref[...].astype(f32)
    scale = lax.rsqrt(jnp.mean(values * values, axis=-1, keepdims=True) + norm_eps)
    normed_ref[...] = (values * scale * gain_ref[...]).astype(bf16)
    weight = weight_ref[...]
    high = weight.astype(bf16).astype(f32)
    middle = (weight - high).astype(bf16).astype(f32)
    notes_ref[...] = jnp.zeros_like(notes_ref)
    notes_ref[0:1, :] = length_ref[...].astype(f32)
    notes_ref[1 : 1 + top, :] = ids_ref[...].astype(f32)
    notes_ref[1 + top : 1 + 2 * top, :] = high
    notes_ref[1 + 2 * top : 1 + 3 * top, :] = middle
    notes_ref[1 + 3 * top : 1 + 4 * top, :] = weight - high - middle
    source = lax.broadcasted_iota(jnp.int32, (requests, LANES), 0)
    lane = lax.broadcasted_iota(jnp.int32, (requests, LANES), 1)
    blocks = notes_ref.shape[0] // NOTES
    for m in range(width):
        start = pl.multiple_of((s ^ m) * part, LANES)
        messages[m][:, :part] = normed_ref[:, pl.ds(start, part)]
        shift = (lane == source + m * requests).astype(bf16)
        for b in range(blocks):
            notes = notes_ref[b * NOTES : (b + 1) * NOTES, :].astype(bf16)
            messages[m][:, part + b * LANES : part + (b + 1) * LANES] = jnp.dot(
                notes, shift, preferred_element_type=f32
            ).astype(bf16)


def prepare(s, hidden, norm_gain, cache_length, expert_ids, expert_weight, width):
    requests, model_width = hidden.shape
    part = model_width // width
    blocks = -(-(1 + 4 * expert_ids.shape[1]) // NOTES)
    message = jax.ShapeDtypeStruct((requests, part + blocks * LANES), bf16)
    return pl.pallas_call(
        functools.partial(prepare_kernel, width),
        in_specs=[smem] + [vmem] * 5,
        out_specs=[vmem] * width,
        out_shape=[message] * width,
        scratch_shapes=[
            pltpu.VMEM((requests, model_width), bf16),
            pltpu.VMEM((blocks * NOTES, requests), f32),
        ],
        compiler_params=pltpu.CompilerParams(vmem_limit_bytes=56 * 2**20),
        cost_estimate=pl.CostEstimate(
            flops=4 * requests * model_width,
            bytes_accessed=4 * requests * model_width + 4 * model_width,
            transcendentals=requests,
        ),
    )(
        s.reshape(1),
        hidden,
        norm_gain.reshape(1, -1),
        cache_length.reshape(1, -1),
        expert_ids.T,
        expert_weight.T,
    )


def message_groups(experts):
    return [[(chunk, n) for chunk in range(CHUNKS)] for n in range(experts)]


def dispatch_kernel(width, experts, top, requests, here_ref, *refs):
    messages = refs[:width]
    groups = message_groups(experts)
    count = len(groups)
    outs, (map_ref, length_ref) = refs[width : width + count], refs[width + count : width + count + 2]
    tokens_ref, select_ref = refs[width + count + 2 :]
    s, e = here_ref[0], here_ref[1]
    part = tokens_ref.shape[1]
    total = width * requests
    piece = CAP_E // CHUNKS
    room = width * piece
    for m in range(width):
        tokens_ref[m * requests : (m + 1) * requests, :] = messages[m][:, :part]
    blocks = (messages[0].shape[1] - part) // LANES
    notes = []
    for b in range(blocks):
        at = part + b * LANES
        summed = messages[0][:, at : at + LANES].astype(f32)
        for m in range(1, width):
            summed = summed + messages[m][:, at : at + LANES].astype(f32)
        notes.append(summed)
    length_ref[...] = notes[0][0:1, :].astype(jnp.int32)

    def note(k):
        at = k % NOTES
        return notes[k // NOTES][at : at + 1, :total]

    rows = max(8, experts)
    expert = (e ^ lax.broadcasted_iota(jnp.int32, (rows, total), 0)).astype(f32)
    hit = jnp.zeros((rows, total), f32)
    share = jnp.zeros((rows, total), f32)
    for t in range(top):
        same = note(1 + t) == expert
        weight = note(1 + top + t) + note(1 + 2 * top + t) + note(1 + 3 * top + t)
        hit = jnp.where(same, 1.0, hit)
        share = share + jnp.where(same, weight, 0.0)
    shift = requests.bit_length() - 1
    a = lax.broadcasted_iota(jnp.int32, (total, total), 0)
    b = lax.broadcasted_iota(jnp.int32, (total, total), 1)
    ahead = ((lax.shift_right_logical(a, shift) == lax.shift_right_logical(b, shift)) & (a < b)).astype(bf16)
    rank = jnp.dot(hit.astype(bf16), ahead, preferred_element_type=f32).astype(jnp.int32)
    lane = lax.broadcasted_iota(jnp.int32, (1, total), 1)
    base = (s ^ lax.shift_right_logical(lane, shift)) * piece
    spot = lax.broadcasted_iota(jnp.int32, (room, total), 0)
    for chunk in range(CHUNKS):
        for n in range(experts):
            local = rank[n : n + 1, :] - chunk * piece
            inside = (hit[n : n + 1, :] > 0.5) & (local >= 0) & (local < piece)
            chosen = jnp.where(inside, base + local, -1) == spot
            at = (chunk * experts + n) * room
            select_ref[at : at + room, :] = jnp.where(chosen, 1.0, 0.0)
            map_ref[at : at + room, :] = jnp.where(chosen, share[n : n + 1, :], 0.0)
    select = select_ref[...].astype(bf16)
    tile = 256 if part % 256 == 0 else LANES
    for at in range(0, part, tile):
        sent = jnp.dot(select, tokens_ref[:, at : at + tile], preferred_element_type=f32)
        for out, group in zip(outs, groups):
            pieces = [
                sent[(chunk * experts + n) * room : (chunk * experts + n + 1) * room, :]
                for chunk, n in group
            ]
            out[:, at : at + tile] = jnp.concatenate(pieces, axis=0).astype(bf16)


def dispatch(s, e, messages, part, experts, top):
    width = len(messages)
    requests = messages[0].shape[0]
    room = width * CAP_E // CHUNKS
    groups = message_groups(experts)
    places = CHUNKS * experts * room
    total = width * requests
    *outs, weight_map, lengths = pl.pallas_call(
        functools.partial(dispatch_kernel, width, experts, top, requests),
        in_specs=[smem] + [vmem] * width,
        out_specs=[vmem] * (len(groups) + 2),
        out_shape=[jax.ShapeDtypeStruct((len(group) * room, part), bf16) for group in groups]
        + [
            jax.ShapeDtypeStruct((places, total), f32),
            jax.ShapeDtypeStruct((1, LANES), jnp.int32),
        ],
        scratch_shapes=[
            pltpu.VMEM((total, part), bf16),
            pltpu.VMEM((places, total), f32),
        ],
        compiler_params=pltpu.CompilerParams(vmem_limit_bytes=16 * 2**20),
        cost_estimate=pl.CostEstimate(
            flops=2 * places * total * part,
            bytes_accessed=2 * part * (total + places),
            transcendentals=0,
        ),
    )(jnp.stack([s, e]).astype(jnp.int32), *messages)
    return outs, weight_map, lengths


def attend_all(queries, caches, lengths):
    scores = [
        lax.dot_general(cache, query, (((0,), (0,)), ((), ())), preferred_element_type=f32)
        for query, cache in zip(queries, caches)
    ]
    probs = []
    for score, length in zip(scores, lengths):
        score = score * score_scale
        places = lax.broadcasted_iota(jnp.int32, score.shape, 0)
        score = jnp.where(places < length, score, -jnp.inf)
        raised = jnp.exp(score - jnp.max(score, axis=0, keepdims=True))
        share = raised * (1.0 / jnp.sum(raised, axis=0, keepdims=True))
        probs.append(share.astype(bf16).T)
    return [
        lax.dot_general(
            prob, cache[:LAT], (((1,), (1,)), ((), ())), preferred_element_type=f32
        ).astype(bf16)
        for prob, cache in zip(probs, caches)
    ]


def attend_cost(count, heads, positions, width):
    return pl.CostEstimate(
        flops=2 * count * heads * positions * (width + LAT),
        bytes_accessed=count * 2 * (heads * width + positions * width + heads * LAT),
        transcendentals=count * heads * positions,
    )


def kept_kernel(step, length_ref, q_ref, c_ref, out_ref):
    i = pl.program_id(0)
    outs = attend_all(
        [q_ref[j] for j in range(step)],
        [c_ref[j] for j in range(step)],
        [length_ref[i * step + j] for j in range(step)],
    )
    for j in range(step):
        out_ref[j] = outs[j]


def attend_kept(queries, cache, lengths):
    count, width, heads = queries.shape
    positions = cache.shape[2]
    step = next(k for k in (8, 4, 2, 1) if count % k == 0)
    return pl.pallas_call(
        functools.partial(kept_kernel, step),
        grid_spec=pltpu.PrefetchScalarGridSpec(
            num_scalar_prefetch=1,
            grid=(count // step,),
            in_specs=[
                pl.BlockSpec((step, width, heads), lambda i, n: (i, 0, 0)),
                pl.BlockSpec((step, width, positions), lambda i, n: (i, 0, 0)),
            ],
            out_specs=pl.BlockSpec((step, heads, LAT), lambda i, n: (i, 0, 0)),
        ),
        out_shape=jax.ShapeDtypeStruct((count, heads, LAT), bf16),
        compiler_params=pltpu.CompilerParams(vmem_limit_bytes=ATTEND_VMEM),
        cost_estimate=attend_cost(count, heads, positions, width),
    )(lengths, queries, cache)


def lent_kernel(lent, index_ref, length_ref, *refs):
    outs = attend_all(
        [refs[i][0] for i in range(lent)],
        [refs[lent + i][0] for i in range(lent)],
        [length_ref[i] for i in range(lent)],
    )
    for i in range(lent):
        refs[2 * lent + i][...] = outs[i]


def attend_lent(queries, cache, index, lengths):
    lent = index.shape[0]
    _, width, heads = queries.shape
    positions = cache.shape[2]

    def at(i):
        return lambda step, idx, n: (idx[i], 0, 0)

    return pl.pallas_call(
        functools.partial(lent_kernel, lent),
        grid_spec=pltpu.PrefetchScalarGridSpec(
            num_scalar_prefetch=2,
            grid=(1,),
            in_specs=[pl.BlockSpec((1, width, heads), at(i)) for i in range(lent)]
            + [pl.BlockSpec((1, width, positions), at(i)) for i in range(lent)],
            out_specs=[pl.BlockSpec((heads, LAT), lambda step, idx, n: (0, 0))] * lent,
        ),
        out_shape=[jax.ShapeDtypeStruct((heads, LAT), bf16)] * lent,
        compiler_params=pltpu.CompilerParams(vmem_limit_bytes=ATTEND_VMEM),
        cost_estimate=attend_cost(lent, heads, positions, width),
    )(index, lengths, *[queries] * lent, *[cache] * lent)


def place_kernel(lent, where_ref, *refs):
    out_ref, sems = refs[lent + 1], refs[lent + 2]
    copies = [
        pltpu.make_async_copy(refs[i], out_ref.at[where_ref[i]], sems.at[i]) for i in range(lent)
    ]
    for copy in copies:
        copy.start()
    for copy in copies:
        copy.wait()


def place(where, taken, kept):
    lent = len(taken)
    return pl.pallas_call(
        functools.partial(place_kernel, lent),
        in_specs=[smem] + [pl.BlockSpec(memory_space=pl.ANY)] * lent + [hbm],
        out_specs=hbm,
        out_shape=jax.ShapeDtypeStruct(kept.shape, kept.dtype),
        scratch_shapes=[pltpu.SemaphoreType.DMA((lent,))],
        input_output_aliases={lent + 1: 0},
        compiler_params=pltpu.CompilerParams(vmem_limit_bytes=2 * 2**20),
    )(where, *taken, kept)


def total_sum(total, width):
    step = 2
    while step < width:
        total = (total.astype(f32) + xor_permute(total, "steal", step).astype(f32)).astype(bf16)
        step *= 2
    return total


def per_device(
    queries,
    latent_cache,
    cache_length,
    steal_source,
    hidden,
    norm_gain,
    expert_ids,
    expert_weight,
    w_gate,
    w_up,
    w_down,
):
    s, e = lax.axis_index("steal"), lax.axis_index("ep")
    width, experts = lax.axis_size("steal"), lax.axis_size("ep")
    requests, model_width = hidden.shape
    top = expert_ids.shape[1]
    part = model_width // width
    core = s % 2
    lent = width - 1

    messages = prepare(s, hidden, norm_gain, cache_length, expert_ids, expert_weight, width)
    messages = [messages[0]] + [xor_permute(messages[m], "steal", m) for m in range(1, width)]
    outgoing, weight_map, peer_lengths = dispatch(s, e, messages, part, experts, top)
    outgoing, peer_lengths = lax.optimization_barrier((outgoing, peer_lengths))
    room = width * CAP_E // CHUNKS
    pieces = {}
    for sent, group in zip(outgoing, message_groups(experts)):
        n = group[0][1]
        got = sent if n == 0 else xor_permute(sent, "ep", n)
        for at, key in enumerate(group):
            pieces[key] = got[at * room : (at + 1) * room]

    slot_ids = jnp.arange(lent, dtype=jnp.int32)
    others = jnp.arange(1, width, dtype=jnp.int32)[:, None]
    peer_lengths = peer_lengths[0, : width * requests].reshape(width, requests)[1:, :lent]
    partner = s ^ ((2 * s - steal_source[:lent]) % width)
    is_partner = partner[None, :] == others
    order = jnp.sum(jnp.where(is_partner, slot_ids[None, :], 0), axis=1)
    lent_lengths = jnp.sum(jnp.where(is_partner, peer_lengths, 0), axis=1)
    comes_from = (s ^ steal_source[:lent])[None, :] == others
    where = jnp.sum(jnp.where(comes_from, slot_ids[None, :], 0), axis=1)
    queries, cache = queries.swapaxes(1, 2), latent_cache.swapaxes(1, 2)
    given = attend_lent(queries, cache, order, lent_lengths)
    lengths, given = lax.optimization_barrier((cache_length, given))
    taken = [xor_permute(given[m - 1], "steal", m) for m in range(1, width)]
    kept = attend_kept(queries, cache, lengths)
    pieces, kept = lax.optimization_barrier((pieces, kept))

    half = w_gate.shape[2] // 2
    gate_send = lax.dynamic_slice(w_gate[0], (0, (1 - core) * half), (part, half))
    gate_keep = lax.dynamic_slice(w_gate[0], (0, core * half), (part, half))
    up_send = lax.dynamic_slice(w_up[0], (0, (1 - core) * half), (part, half))
    up_keep = lax.dynamic_slice(w_up[0], (0, core * half), (part, half))
    down_own = lax.dynamic_slice(w_down[0], (core * half, 0), (half, part))
    down_other = lax.dynamic_slice(w_down[0], ((1 - core) * half, 0), (half, part))

    mixed = jnp.zeros((width * requests, part), f32)
    for chunk in range(CHUNKS):
        arrived = [pieces[chunk, n] for n in range(experts)]
        arrived = jnp.concatenate(arrived, axis=0)
        send = jnp.concatenate(
            [
                jnp.dot(arrived, gate_send, preferred_element_type=f32).astype(bf16),
                jnp.dot(arrived, up_send, preferred_element_type=f32).astype(bf16),
            ],
            axis=1,
        )
        got = xor_permute(send, "steal", 1)
        keep = jnp.concatenate(
            [
                jnp.dot(arrived, gate_keep, preferred_element_type=f32),
                jnp.dot(arrived, up_keep, preferred_element_type=f32),
            ],
            axis=1,
        )
        total = (keep + got.astype(f32)).astype(bf16)
        if chunk == 0:
            total, taken = lax.optimization_barrier((total, taken))
        total = total_sum(total, width)
        if chunk == 0:
            attended = place(where, taken, kept)
            total, attended = lax.optimization_barrier((total, attended))
        total = total.astype(f32)
        active = (jax.nn.silu(total[:, :half]) * total[:, half:]).astype(bf16)
        other = xor_permute(active, "steal", 1)
        produced = (
            jnp.dot(active, down_own, preferred_element_type=f32)
            + jnp.dot(other, down_other, preferred_element_type=f32)
        ).astype(bf16)
        produced = produced.reshape(experts, room, part)
        returned = jnp.concatenate(
            [produced[0]] + [xor_permute(produced[n], "ep", n) for n in range(1, experts)],
            axis=0,
        )
        mixed = mixed + jnp.einsum(
            "ir,ik->rk",
            weight_map[chunk * experts * room : (chunk + 1) * experts * room],
            returned.astype(f32),
            precision=lax.Precision.HIGHEST,
            preferred_element_type=f32,
        )
    mixed = mixed.astype(bf16).reshape(width, requests, part)
    result = jnp.zeros((requests, model_width), bf16)
    for m in range(width):
        got = mixed[m] if m == 0 else xor_permute(mixed[m], "steal", m)
        result = lax.dynamic_update_slice(result, got, (0, (s ^ m) * part))
    return (attended, result)


def solution(mesh):
    return jax.shard_map(
        per_device,
        mesh=mesh,
        in_specs=(
            P(("rep", "steal", "ep"), None, None),
            P(("rep", "steal", "ep"), None, None),
            P(("rep", "steal", "ep")),
            P(("rep", "steal", "ep")),
            P(("rep", "steal", "ep"), None),
            P(),
            P(("rep", "steal", "ep"), None),
            P(("rep", "steal", "ep"), None),
            P("ep", "steal", None),
            P("ep", "steal", None),
            P("ep", None, "steal"),
        ),
        out_specs=(P(("rep", "steal", "ep"), None, None), P(("rep", "steal", "ep"), None)),
        check_vma=False,
    )
```

time: 105 us -> 73.1 us (0.70)
  the two profiles are of different devices: /device:TPU:17 before, /device:TPU:0 now
where the time goes in v2:
time: 73.1 us; the launch traced here: 72.9 us
  waiting for transfers between devices  25.8 us (35%)
  starting transfers between devices  24.8 us (34%)
  Pallas kernels  8.62 us (12%)
  matrix products  6.08 us (8%)
  local copies, waits for them, and re-layouts  5.19 us (7%)
  other arithmetic  1.32 us (2%)
  between operations  1.01 us (1%)
    ppermute x24, waiting for transfers between devices, xor_permute(): return lax.ppermute(x, axis, [(i, i ^ m) for i in range(size)])  25.8 us
    ppermute x24, starting transfers between devices, xor_permute(): return lax.ppermute(x, axis, [(i, i ^ m) for i in range(size)])  24.8 us
    unnamed x24, local copies, waits for them, and re-layouts  4.91 us
    pallas_call x1, Pallas kernels, attend_kept(): pl.pallas_call(functools.partial(kept_kernel, step), grid_spec=pltpu.Pref...  3.27 us
    pallas_call x1, Pallas kernels, prepare(): pl.pallas_call(functools.partial(prepare_kernel, width), in_specs=[smem]...  1.88 us
  transfers between devices with their start and end apart: 24, of which 10 were waited for; matrix products, arithmetic and copies ran while one was open for 10% of the time, Pallas kernels for 8%

profile of v2, /device:TPU:0, one launch (start us, length us, event | category | flops | bytes accessed | tf_op | source)
XLA Modules:
  0.0 72.9 jit_solution(6422996841239188301)
XLA Ops:
  0.6 1.9 %shard_map.122 = (bf16[16,1920]{1,0:T(8,128)(2,1)}, bf16[16,1920]{1,0:T(8,128)(2,1)}, bf16[16,1920]{1,0:T(8,128)(2,1)}, bf16[16,1920]{1,0:T(8,128)(2,1)}) custom-call(s32[1]{0:T(128)} %bitcast.here_ref, bf16[16,7168]{1,0:T(8,128)(2,1)} %hidden_ref.1, f32[1,7168]{1,0:T(1,128)} %bitcast.67, s32[1,16]{1,0:T(1,128)} %bitcast.66, s32[2,16]{1,0:T(2,128)} %bitcast.68, ...), custom_call_target="tpu_custom_call" | custom-call | flops 458752 | bytes 487424 | tf_op jit(solution)/shard_map/pallas_call | solution.py:70
  3.0 2.5 %collective-permute-start.1 = (bf16[16,1920]{1,0:T(8,128)(2,1)}, bf16[16,1920]{1,0:T(8,128)(2,1)S(1)}, u32[]{:S(2)}, u32[]{:S(2)}) collective-permute-start(bf16[16,1920]{1,0:T(8,128)(2,1)} %get-tuple-element.41), channel_id=1, source_target_pairs={{0,8},{4,12},{8,0},{12,4},{1,9},{5,13},{9,1},{13,5},{2,10},{6,14},... | collective-permute-start | bytes 184328 | tf_op jit(solution)/shard_map/ppermute | solution.py:28
  6.4 2.0 %collective-permute-done.1.refs_2_ = bf16[16,1920]{1,0:T(8,128)(2,1)S(1)} collective-permute-done((bf16[16,1920]{1,0:T(8,128)(2,1)}, bf16[16,1920]{1,0:T(8,128)(2,1)S(1)}, u32[]{:S(2)}, u32[]{:S(2)}) %collective-permute-start.1) | collective-permute-done | bytes 61472 | tf_op jit(solution)/shard_map/ppermute | solution.py:28
  8.3 1.4 %collective-permute-done.2.refs_3_ = bf16[16,1920]{1,0:T(8,128)(2,1)S(1)} collective-permute-done((bf16[16,1920]{1,0:T(8,128)(2,1)}, bf16[16,1920]{1,0:T(8,128)(2,1)S(1)}, u32[]{:S(2)}, u32[]{:S(2)}) %collective-permute-start.2) | collective-permute-done | bytes 61472 | tf_op jit(solution)/shard_map/ppermute | solution.py:28
  11.6 1.6 %collective-permute-start.3 = (bf16[48,1792]{1,0:T(8,128)(2,1)S(1)}, bf16[48,1792]{1,0:T(8,128)(2,1)S(1)}, u32[]{:S(2)}, u32[]{:S(2)}) collective-permute-start(bf16[48,1792]{1,0:T(8,128)(2,1)S(1)} %get-tuple-element.49), channel_id=1, source_target_pairs={{0,1},{1,0},{2,3},{3,2},{4,5},{5,4},{6,7},{7,6},{8,9},{9,8},{10,11... | collective-permute-start | bytes 516104 | tf_op jit(solution)/shard_map/ppermute | solution.py:28
  13.2 2.6 %collective-permute-start.4 = (bf16[48,1792]{1,0:T(8,128)(2,1)S(1)}, bf16[48,1792]{1,0:T(8,128)(2,1)S(1)}, u32[]{:S(2)}, u32[]{:S(2)}) collective-permute-start(bf16[48,1792]{1,0:T(8,128)(2,1)S(1)} %get-tuple-element.50), channel_id=1, source_target_pairs={{0,2},{1,3},{2,0},{3,1},{4,6},{5,7},{6,4},{7,5},{8,10},{9,11},{10,... | collective-permute-start | bytes 516104 | tf_op jit(solution)/shard_map/ppermute | solution.py:28
  16.4 1.7 %copy-done = bf16[16,128,576]{1,2,0:T(8,128)(2,1)S(1)} copy-done((bf16[16,128,576]{1,2,0:T(8,128)(2,1)S(1)}, bf16[16,128,576]{1,2,0:T(8,128)(2,1)}, u32[]{:S(2)}) %copy-start) | copy-done | bytes 2359320
  18.0 1.7 %copy-done.2 = bf16[16,128,576]{1,2,0:T(8,128)(2,1)S(1)} copy-done((bf16[16,128,576]{1,2,0:T(8,128)(2,1)S(1)}, bf16[16,128,576]{1,2,0:T(8,128)(2,1)}, u32[]{:S(2)}) %copy-start.2) | copy-done | bytes 2359320
  19.7 1.2 %shard_map.124 = (bf16[128,512]{1,0:T(8,128)(2,1)S(1)}, bf16[128,512]{1,0:T(8,128)(2,1)S(1)}, bf16[128,512]{1,0:T(8,128)(2,1)S(1)}) custom-call(s32[3]{0:T(128)S(1)} %get-tuple-element.77.index_ref, s32[3]{0:T(128)S(1)} %get-tuple-element.76.length_ref, bf16[16,576,128]{2,1,0:T(8,128)(2,1)S(1)} %bitcast.58, bf16[16,576,128]{2,1,0:T(8,128)(2,1)S(1)} %bitcast.59, ...), custom_call_target="tpu_custom_call" | custom-call | flops 106954752 | bytes 1277952 | tf_op jit(solution)/shard_map/pallas_call | solution.py:272
  20.9 1.3 %collective-permute-start.8 = (bf16[128,512]{1,0:T(8,128)(2,1)S(1)}, bf16[128,512]{1,0:T(8,128)(2,1)S(1)}, u32[]{:S(2)}, u32[]{:S(2)}) collective-permute-start(bf16[128,512]{1,0:T(8,128)(2,1)S(1)} %get-tuple-element.62), channel_id=1, source_target_pairs={{0,8},{4,12},{8,0},{12,4},{1,9},{5,13},{9,1},{13,5},{2,10},{6,14},... | collective-permute-start | bytes 393224 | tf_op jit(solution)/shard_map/ppermute | solution.py:28
  22.3 3.3 %shard_map.125.refs_3_ = bf16[16,128,512]{2,1,0:T(8,128)(2,1)} custom-call(s32[16]{0:T(128)S(1)} %copy-done.4, bf16[16,576,128]{2,1,0:T(8,128)(2,1)S(1)} %bitcast.61, bf16[16,576,128]{2,1,0:T(8,128)(2,1)S(1)} %bitcast.65), custom_call_target="tpu_custom_call" | custom-call | flops 570425344 | bytes 6815744 | tf_op jit(solution)/shard_map/pallas_call | solution.py:237
  26.1 2.6 %collective-permute-done.4 = bf16[48,1792]{1,0:T(8,128)(2,1)S(1)} collective-permute-done((bf16[48,1792]{1,0:T(8,128)(2,1)S(1)}, bf16[48,1792]{1,0:T(8,128)(2,1)S(1)}, u32[]{:S(2)}, u32[]{:S(2)}) %collective-permute-start.4) | collective-permute-done | bytes 172064 | tf_op jit(solution)/shard_map/ppermute | solution.py:28
  33.7 1.3 %collective-permute-start.10 = (bf16[96,1024]{1,0:T(8,128)(2,1)S(1)}, bf16[96,1024]{1,0:T(8,128)(2,1)S(1)}, u32[]{:S(2)}, u32[]{:S(2)}) collective-permute-start(bf16[96,1024]{1,0:T(8,128)(2,1)S(1)} %fusion.49), channel_id=1, source_target_pairs={{0,8},{4,12},{8,0},{12,4},{1,9},{5,13},{9,1},{13,5},{2,10},{6,14},... | collective-permute-start | bytes 589832 | tf_op jit(solution)/shard_map/ppermute | solution.py:28
  35.9 1.3 %shard_map.126 = bf16[16,128,512]{2,1,0:T(8,128)(2,1)} custom-call(s32[3]{0:T(128)S(1)} %get-tuple-element.78.where_ref, bf16[128,512]{1,0:T(8,128)(2,1)S(1)} %collective-permute-done.7.refs_0_, bf16[128,512]{1,0:T(8,128)(2,1)S(1)} %collective-permute-done.8.refs_1_, ...), custom_call_target="tpu_custom_call", output_to_operand_aliasing={{}: (4, {})} | custom-call | tf_op jit(solution)/shard_map/pallas_call | solution.py:300
  37.2 4.3 %collective-permute-done.10 = bf16[96,1024]{1,0:T(8,128)(2,1)S(1)} collective-permute-done((bf16[96,1024]{1,0:T(8,128)(2,1)S(1)}, bf16[96,1024]{1,0:T(8,128)(2,1)S(1)}, u32[]{:S(2)}, u32[]{:S(2)}) %collective-permute-start.10) | collective-permute-done | bytes 196640 | tf_op jit(solution)/shard_map/ppermute | solution.py:28
  41.5 3.4 %collective-permute-done.16 = bf16[96,1024]{1,0:T(8,128)(2,1)S(1)} collective-permute-done((bf16[96,1024]{1,0:T(8,128)(2,1)S(1)}, bf16[96,1024]{1,0:T(8,128)(2,1)S(1)}, u32[]{:S(2)}, u32[]{:S(2)}) %collective-permute-start.16) | collective-permute-done | bytes 196640 | tf_op jit(solution)/shard_map/ppermute | solution.py:28
  47.1 2.5 %collective-permute-start.20 = (bf16[24,1792]{1,0:T(8,128)(2,1)S(1)}, bf16[24,1792]{1,0:T(8,128)(2,1)S(1)}, u32[]{:S(2)}, u32[]{:S(2)}) collective-permute-start(bf16[24,1792]{1,0:T(8,128)(2,1)S(1)} %get-tuple-element.84), channel_id=1, source_target_pairs={{0,3},{1,2},{2,1},{3,0},{4,7},{5,6},{6,5},{7,4},{8,11},{9,10},{10,... | collective-permute-start | bytes 258056 | tf_op jit(solution)/shard_map/ppermute | solution.py:28
  49.7 2.1 %collective-permute-start.19 = (bf16[24,1792]{1,0:T(8,128)(2,1)S(1)}, bf16[24,1792]{1,0:T(8,128)(2,1)S(1)}, u32[]{:S(2)}, u32[]{:S(2)}) collective-permute-start(bf16[24,1792]{1,0:T(8,128)(2,1)S(1)} %get-tuple-element.85), channel_id=1, source_target_pairs={{0,2},{1,3},{2,0},{3,1},{4,6},{5,7},{6,4},{7,5},{8,10},{9,11},{10,... | collective-permute-start | bytes 258056 | tf_op jit(solution)/shard_map/ppermute | solution.py:28
  52.3 2.4 %collective-permute-start.14 = (bf16[24,1792]{1,0:T(8,128)(2,1)S(1)}, bf16[24,1792]{1,0:T(8,128)(2,1)S(1)}, u32[]{:S(2)}, u32[]{:S(2)}) collective-permute-start(bf16[24,1792]{1,0:T(8,128)(2,1)S(1)} %get-tuple-element.80), channel_id=1, source_target_pairs={{0,3},{1,2},{2,1},{3,0},{4,7},{5,6},{6,5},{7,4},{8,11},{9,10},{10,... | collective-permute-start | bytes 258056 | tf_op jit(solution)/shard_map/ppermute | solution.py:28
  55.8 1.8 %collective-permute-start.12 = (bf16[24,1792]{1,0:T(8,128)(2,1)S(1)}, bf16[24,1792]{1,0:T(8,128)(2,1)S(1)}, u32[]{:S(2)}, u32[]{:S(2)}) collective-permute-start(bf16[24,1792]{1,0:T(8,128)(2,1)S(1)} %get-tuple-element.82), channel_id=1, source_target_pairs={{0,1},{1,0},{2,3},{3,2},{4,5},{5,4},{6,7},{7,6},{8,9},{9,8},{10,11... | collective-permute-start | bytes 258056 | tf_op jit(solution)/shard_map/ppermute | solution.py:28
  57.6 5.2 %collective-permute-done.19 = bf16[24,1792]{1,0:T(8,128)(2,1)S(1)} collective-permute-done((bf16[24,1792]{1,0:T(8,128)(2,1)S(1)}, bf16[24,1792]{1,0:T(8,128)(2,1)S(1)}, u32[]{:S(2)}, u32[]{:S(2)}) %collective-permute-start.19) | collective-permute-done | bytes 86048 | tf_op jit(solution)/shard_map/ppermute | solution.py:28
  63.2 3.2 %collective-permute-done.13 = bf16[24,1792]{1,0:T(8,128)(2,1)S(1)} collective-permute-done((bf16[24,1792]{1,0:T(8,128)(2,1)S(1)}, bf16[24,1792]{1,0:T(8,128)(2,1)S(1)}, u32[]{:S(2)}, u32[]{:S(2)}) %collective-permute-start.13) | collective-permute-done | bytes 86048 | tf_op jit(solution)/shard_map/ppermute | solution.py:28
  66.9 1.3 %collective-permute-start.22 = (bf16[16,1792]{1,0:T(8,128)(2,1)S(1)}, bf16[16,1792]{1,0:T(8,128)(2,1)S(1)}, u32[]{:S(2)}, u32[]{:S(2)}) collective-permute-start(bf16[16,1792]{1,0:T(8,128)(2,1)S(1)} %get-tuple-element.88), channel_id=1, source_target_pairs={{0,8},{4,12},{8,0},{12,4},{1,9},{5,13},{9,1},{13,5},{2,10},{6,14},... | collective-permute-start | bytes 172040 | tf_op jit(solution)/shard_map/ppermute | solution.py:28
  68.8 2.5 %collective-permute-done.22 = bf16[16,1792]{1,0:T(8,128)(2,1)S(1)} collective-permute-done((bf16[16,1792]{1,0:T(8,128)(2,1)S(1)}, bf16[16,1792]{1,0:T(8,128)(2,1)S(1)}, u32[]{:S(2)}, u32[]{:S(2)}) %collective-permute-start.22) | collective-permute-done | bytes 57376 | tf_op jit(solution)/shard_map/ppermute | solution.py:28
  (94 shorter events, 16.8 us)
Async XLA Ops:
  2.5 3.9 %collective-permute-start = (bf16[16,1920]{1,0:T(8,128)(2,1)}, bf16[16,1920]{1,0:T(8,128)(2,1)S(1)}, u32[]{:S(2)}, u32[]{:S(2)}) collective-permute-start(bf16[16,1920]{1,0:T(8,128)(2,1)} %get-tuple-element.40), channel_id=1, source_target_pairs={{0,4},{4,0},{8,12},{12,8},{1,5},{5,1},{9,13},{13,9},{2,6},{6,2},{1... | collective-permute-start | bytes 184328 | tf_op jit(solution)/shard_map/ppermute | solution.py:28
  3.0 5.4 %collective-permute-start.1 = (bf16[16,1920]{1,0:T(8,128)(2,1)}, bf16[16,1920]{1,0:T(8,128)(2,1)S(1)}, u32[]{:S(2)}, u32[]{:S(2)}) collective-permute-start(bf16[16,1920]{1,0:T(8,128)(2,1)} %get-tuple-element.41), channel_id=1, source_target_pairs={{0,8},{4,12},{8,0},{12,4},{1,9},{5,13},{9,1},{13,5},{2,10},{6,14},... | collective-permute-start | bytes 184328 | tf_op jit(solution)/shard_map/ppermute | solution.py:28
  5.5 4.2 %collective-permute-start.2 = (bf16[16,1920]{1,0:T(8,128)(2,1)}, bf16[16,1920]{1,0:T(8,128)(2,1)S(1)}, u32[]{:S(2)}, u32[]{:S(2)}) collective-permute-start(bf16[16,1920]{1,0:T(8,128)(2,1)} %get-tuple-element.42), channel_id=1, source_target_pairs={{0,12},{4,8},{8,4},{12,0},{1,13},{5,9},{9,5},{13,1},{2,14},{6,10},... | collective-permute-start | bytes 184328 | tf_op jit(solution)/shard_map/ppermute | solution.py:28
  11.6 14.0 %collective-permute-start.3 = (bf16[48,1792]{1,0:T(8,128)(2,1)S(1)}, bf16[48,1792]{1,0:T(8,128)(2,1)S(1)}, u32[]{:S(2)}, u32[]{:S(2)}) collective-permute-start(bf16[48,1792]{1,0:T(8,128)(2,1)S(1)} %get-tuple-element.49), channel_id=1, source_target_pairs={{0,1},{1,0},{2,3},{3,2},{4,5},{5,4},{6,7},{7,6},{8,9},{9,8},{10,11... | collective-permute-start | bytes 516104 | tf_op jit(solution)/shard_map/ppermute | solution.py:28
  13.2 15.5 %collective-permute-start.4 = (bf16[48,1792]{1,0:T(8,128)(2,1)S(1)}, bf16[48,1792]{1,0:T(8,128)(2,1)S(1)}, u32[]{:S(2)}, u32[]{:S(2)}) collective-permute-start(bf16[48,1792]{1,0:T(8,128)(2,1)S(1)} %get-tuple-element.50), channel_id=1, source_target_pairs={{0,2},{1,3},{2,0},{3,1},{4,6},{5,7},{6,4},{7,5},{8,10},{9,11},{10,... | collective-permute-start | bytes 516104 | tf_op jit(solution)/shard_map/ppermute | solution.py:28
  15.8 13.0 %collective-permute-start.5 = (bf16[48,1792]{1,0:T(8,128)(2,1)S(1)}, bf16[48,1792]{1,0:T(8,128)(2,1)S(1)}, u32[]{:S(2)}, u32[]{:S(2)}) collective-permute-start(bf16[48,1792]{1,0:T(8,128)(2,1)S(1)} %get-tuple-element.51), channel_id=1, source_target_pairs={{0,3},{1,2},{2,1},{3,0},{4,7},{5,6},{6,5},{7,4},{8,11},{9,10},{10,... | collective-permute-start | bytes 516104 | tf_op jit(solution)/shard_map/ppermute | solution.py:28
  20.9 12.8 %collective-permute-start.7 = (bf16[128,512]{1,0:T(8,128)(2,1)S(1)}, bf16[128,512]{1,0:T(8,128)(2,1)S(1)}, u32[]{:S(2)}, u32[]{:S(2)}) collective-permute-start(bf16[128,512]{1,0:T(8,128)(2,1)S(1)} %get-tuple-element.61), channel_id=1, source_target_pairs={{0,4},{4,0},{8,12},{12,8},{1,5},{5,1},{9,13},{13,9},{2,6},{6,2},{1... | collective-permute-start | bytes 393224 | tf_op jit(solution)/shard_map/ppermute | solution.py:28
  20.9 12.7 %collective-permute-start.8 = (bf16[128,512]{1,0:T(8,128)(2,1)S(1)}, bf16[128,512]{1,0:T(8,128)(2,1)S(1)}, u32[]{:S(2)}, u32[]{:S(2)}) collective-permute-start(bf16[128,512]{1,0:T(8,128)(2,1)S(1)} %get-tuple-element.62), channel_id=1, source_target_pairs={{0,8},{4,12},{8,0},{12,4},{1,9},{5,13},{9,1},{13,5},{2,10},{6,14},... | collective-permute-start | bytes 393224 | tf_op jit(solution)/shard_map/ppermute | solution.py:28
  25.5 8.1 %collective-permute-start.9 = (bf16[128,512]{1,0:T(8,128)(2,1)S(1)}, bf16[128,512]{1,0:T(8,128)(2,1)S(1)}, u32[]{:S(2)}, u32[]{:S(2)}) collective-permute-start(bf16[128,512]{1,0:T(8,128)(2,1)S(1)} %get-tuple-element.63), channel_id=1, source_target_pairs={{0,12},{4,8},{8,4},{12,0},{1,13},{5,9},{9,5},{13,1},{2,14},{6,10},... | collective-permute-start | bytes 393224 | tf_op jit(solution)/shard_map/ppermute | solution.py:28
  32.1 1.5 %collective-permute-start.6 = (bf16[96,1024]{1,0:T(8,128)(2,1)S(1)}, bf16[96,1024]{1,0:T(8,128)(2,1)S(1)}, u32[]{:S(2)}, u32[]{:S(2)}) collective-permute-start(bf16[96,1024]{1,0:T(8,128)(2,1)S(1)} %pad_maximum_fusion), channel_id=1, source_target_pairs={{0,4},{4,0},{8,12},{12,8},{1,5},{5,1},{9,13},{13,9},{2,6},{6,2},{1... | collective-permute-start | bytes 589832 | tf_op jit(solution)/shard_map/ppermute | solution.py:28
  32.2 2.8 %collective-permute-start.15 = (bf16[96,1024]{1,0:T(8,128)(2,1)S(1)}, bf16[96,1024]{1,0:T(8,128)(2,1)S(1)}, u32[]{:S(2)}, u32[]{:S(2)}) collective-permute-start(bf16[96,1024]{1,0:T(8,128)(2,1)S(1)} %pad_maximum_fusion.1), channel_id=1, source_target_pairs={{0,4},{4,0},{8,12},{12,8},{1,5},{5,1},{9,13},{13,9},{2,6},{6,2},{1... | collective-permute-start | bytes 589832 | tf_op jit(solution)/shard_map/ppermute | solution.py:28
  33.7 7.8 %collective-permute-start.10 = (bf16[96,1024]{1,0:T(8,128)(2,1)S(1)}, bf16[96,1024]{1,0:T(8,128)(2,1)S(1)}, u32[]{:S(2)}, u32[]{:S(2)}) collective-permute-start(bf16[96,1024]{1,0:T(8,128)(2,1)S(1)} %fusion.49), channel_id=1, source_target_pairs={{0,8},{4,12},{8,0},{12,4},{1,9},{5,13},{9,1},{13,5},{2,10},{6,14},... | collective-permute-start | bytes 589832 | tf_op jit(solution)/shard_map/ppermute | solution.py:28
  35.0 9.9 %collective-permute-start.16 = (bf16[96,1024]{1,0:T(8,128)(2,1)S(1)}, bf16[96,1024]{1,0:T(8,128)(2,1)S(1)}, u32[]{:S(2)}, u32[]{:S(2)}) collective-permute-start(bf16[96,1024]{1,0:T(8,128)(2,1)S(1)} %fusion.50), channel_id=1, source_target_pairs={{0,8},{4,12},{8,0},{12,4},{1,9},{5,13},{9,1},{13,5},{2,10},{6,14},... | collective-permute-start | bytes 589832 | tf_op jit(solution)/shard_map/ppermute | solution.py:28
  45.0 1.6 %collective-permute-start.17 = (bf16[96,512]{1,0:T(8,128)(2,1)S(1)}, bf16[96,512]{1,0:T(8,128)(2,1)S(1)}, u32[]{:S(2)}, u32[]{:S(2)}) collective-permute-start(bf16[96,512]{1,0:T(8,128)(2,1)S(1)} %fusion.67), channel_id=1, source_target_pairs={{0,4},{4,0},{8,12},{12,8},{1,5},{5,1},{9,13},{13,9},{2,6},{6,2},{1... | collective-permute-start | bytes 294920 | tf_op jit(solution)/shard_map/ppermute | solution.py:28
  46.1 5.8 %collective-permute-start.11 = (bf16[96,512]{1,0:T(8,128)(2,1)S(1)}, bf16[96,512]{1,0:T(8,128)(2,1)S(1)}, u32[]{:S(2)}, u32[]{:S(2)}) collective-permute-start(bf16[96,512]{1,0:T(8,128)(2,1)S(1)} %fusion.68), channel_id=1, source_target_pairs={{0,4},{4,0},{8,12},{12,8},{1,5},{5,1},{9,13},{13,9},{2,6},{6,2},{1... | collective-permute-start | bytes 294920 | tf_op jit(solution)/shard_map/ppermute | solution.py:28
  47.1 8.7 %collective-permute-start.20 = (bf16[24,1792]{1,0:T(8,128)(2,1)S(1)}, bf16[24,1792]{1,0:T(8,128)(2,1)S(1)}, u32[]{:S(2)}, u32[]{:S(2)}) collective-permute-start(bf16[24,1792]{1,0:T(8,128)(2,1)S(1)} %get-tuple-element.84), channel_id=1, source_target_pairs={{0,3},{1,2},{2,1},{3,0},{4,7},{5,6},{6,5},{7,4},{8,11},{9,10},{10,... | collective-permute-start | bytes 258056 | tf_op jit(solution)/shard_map/ppermute | solution.py:28
  49.7 13.1 %collective-permute-start.19 = (bf16[24,1792]{1,0:T(8,128)(2,1)S(1)}, bf16[24,1792]{1,0:T(8,128)(2,1)S(1)}, u32[]{:S(2)}, u32[]{:S(2)}) collective-permute-start(bf16[24,1792]{1,0:T(8,128)(2,1)S(1)} %get-tuple-element.85), channel_id=1, source_target_pairs={{0,2},{1,3},{2,0},{3,1},{4,6},{5,7},{6,4},{7,5},{8,10},{9,11},{10,... | collective-permute-start | bytes 258056 | tf_op jit(solution)/shard_map/ppermute | solution.py:28
  51.8 11.0 %collective-permute-start.18 = (bf16[24,1792]{1,0:T(8,128)(2,1)S(1)}, bf16[24,1792]{1,0:T(8,128)(2,1)S(1)}, u32[]{:S(2)}, u32[]{:S(2)}) collective-permute-start(bf16[24,1792]{1,0:T(8,128)(2,1)S(1)} %get-tuple-element.86), channel_id=1, source_target_pairs={{0,1},{1,0},{2,3},{3,2},{4,5},{5,4},{6,7},{7,6},{8,9},{9,8},{10,11... | collective-permute-start | bytes 258056 | tf_op jit(solution)/shard_map/ppermute | solution.py:28
  52.3 10.8 %collective-permute-start.14 = (bf16[24,1792]{1,0:T(8,128)(2,1)S(1)}, bf16[24,1792]{1,0:T(8,128)(2,1)S(1)}, u32[]{:S(2)}, u32[]{:S(2)}) collective-permute-start(bf16[24,1792]{1,0:T(8,128)(2,1)S(1)} %get-tuple-element.80), channel_id=1, source_target_pairs={{0,3},{1,2},{2,1},{3,0},{4,7},{5,6},{6,5},{7,4},{8,11},{9,10},{10,... | collective-permute-start | bytes 258056 | tf_op jit(solution)/shard_map/ppermute | solution.py:28
  54.8 11.6 %collective-permute-start.13 = (bf16[24,1792]{1,0:T(8,128)(2,1)S(1)}, bf16[24,1792]{1,0:T(8,128)(2,1)S(1)}, u32[]{:S(2)}, u32[]{:S(2)}) collective-permute-start(bf16[24,1792]{1,0:T(8,128)(2,1)S(1)} %get-tuple-element.81), channel_id=1, source_target_pairs={{0,2},{1,3},{2,0},{3,1},{4,6},{5,7},{6,4},{7,5},{8,10},{9,11},{10,... | collective-permute-start | bytes 258056 | tf_op jit(solution)/shard_map/ppermute | solution.py:28
  55.8 10.6 %collective-permute-start.12 = (bf16[24,1792]{1,0:T(8,128)(2,1)S(1)}, bf16[24,1792]{1,0:T(8,128)(2,1)S(1)}, u32[]{:S(2)}, u32[]{:S(2)}) collective-permute-start(bf16[24,1792]{1,0:T(8,128)(2,1)S(1)} %get-tuple-element.82), channel_id=1, source_target_pairs={{0,1},{1,0},{2,3},{3,2},{4,5},{5,4},{6,7},{7,6},{8,9},{9,8},{10,11... | collective-permute-start | bytes 258056 | tf_op jit(solution)/shard_map/ppermute | solution.py:28
  66.8 1.9 %collective-permute-start.21 = (bf16[16,1792]{1,0:T(8,128)(2,1)S(1)}, bf16[16,1792]{1,0:T(8,128)(2,1)S(1)}, u32[]{:S(2)}, u32[]{:S(2)}) collective-permute-start(bf16[16,1792]{1,0:T(8,128)(2,1)S(1)} %get-tuple-element.89), channel_id=1, source_target_pairs={{0,4},{4,0},{8,12},{12,8},{1,5},{5,1},{9,13},{13,9},{2,6},{6,2},{1... | collective-permute-start | bytes 172040 | tf_op jit(solution)/shard_map/ppermute | solution.py:28
  66.9 4.4 %collective-permute-start.22 = (bf16[16,1792]{1,0:T(8,128)(2,1)S(1)}, bf16[16,1792]{1,0:T(8,128)(2,1)S(1)}, u32[]{:S(2)}, u32[]{:S(2)}) collective-permute-start(bf16[16,1792]{1,0:T(8,128)(2,1)S(1)} %get-tuple-element.88), channel_id=1, source_target_pairs={{0,8},{4,12},{8,0},{12,4},{1,9},{5,13},{9,1},{13,5},{2,10},{6,14},... | collective-permute-start | bytes 172040 | tf_op jit(solution)/shard_map/ppermute | solution.py:28
  68.2 3.9 %collective-permute-start.23 = (bf16[16,1792]{1,0:T(8,128)(2,1)S(1)}, bf16[16,1792]{1,0:T(8,128)(2,1)S(1)}, u32[]{:S(2)}, u32[]{:S(2)}) collective-permute-start(bf16[16,1792]{1,0:T(8,128)(2,1)S(1)} %get-tuple-element.87), channel_id=1, source_target_pairs={{0,12},{4,8},{8,4},{12,0},{1,13},{5,9},{9,5},{13,1},{2,14},{6,10},... | collective-permute-start | bytes 172040 | tf_op jit(solution)/shard_map/ppermute | solution.py:28
  (9 other events, 29.6 us)

commit v3 on v2

--- a/solution.py
+++ b/solution.py
@@ -9,7 +9,7 @@
 
 LAT = 512
 CAP_E = 12
-CHUNKS = 2
+CORES = 2
 LANES = 128
 ATTEND_VMEM = 12 * 2**20
 NOTES = 16
@@ -21,6 +21,8 @@
 vmem = pl.BlockSpec(memory_space=pltpu.VMEM)
 hbm = pl.BlockSpec(memory_space=pltpu.HBM)
 smem = pl.BlockSpec(memory_space=pltpu.SMEM)
+
+little = pl.CostEstimate(flops=0, bytes_accessed=0, transcendentals=0)
 
 
 def xor_permute(x, axis, m):
@@ -77,11 +79,7 @@
             pltpu.VMEM((blocks * NOTES, requests), f32),
         ],
         compiler_params=pltpu.CompilerParams(vmem_limit_bytes=56 * 2**20),
-        cost_estimate=pl.CostEstimate(
-            flops=4 * requests * model_width,
-            bytes_accessed=4 * requests * model_width + 4 * model_width,
-            transcendentals=requests,
-        ),
+        cost_estimate=little,
     )(
         s.reshape(1),
         hidden,
@@ -92,30 +90,20 @@
     )
 
 
-def message_groups(experts):
-    return [[(chunk, n) for chunk in range(CHUNKS)] for n in range(experts)]
-
-
-def dispatch_kernel(width, experts, top, requests, here_ref, *refs):
-    messages = refs[:width]
-    groups = message_groups(experts)
-    count = len(groups)
-    outs, (map_ref, length_ref) = refs[width : width + count], refs[width + count : width + count + 2]
-    tokens_ref, select_ref = refs[width + count + 2 :]
+def dispatch_kernel(senders, experts, top, requests, here_ref, *refs):
+    messages, refs = refs[:senders], refs[senders:]
+    outs, (map_ref, length_ref, tokens_ref, select_ref) = refs[:experts], refs[experts:]
     s, e = here_ref[0], here_ref[1]
     part = tokens_ref.shape[1]
-    total = width * requests
-    piece = CAP_E // CHUNKS
-    room = width * piece
-    for m in range(width):
-        tokens_ref[m * requests : (m + 1) * requests, :] = messages[m][:, :part]
-    blocks = (messages[0].shape[1] - part) // LANES
+    total = senders * requests
+    room = senders * CAP_E
+    for i in range(senders):
+        tokens_ref[i * requests : (i + 1) * requests, :] = messages[i][:, :part]
     notes = []
-    for b in range(blocks):
-        at = part + b * LANES
+    for at in range(part, messages[0].shape[1], LANES):
         summed = messages[0][:, at : at + LANES].astype(f32)
-        for m in range(1, width):
-            summed = summed + messages[m][:, at : at + LANES].astype(f32)
+        for i in range(1, senders):
+            summed = summed + messages[i][:, at : at + LANES].astype(f32)
         notes.append(summed)
     length_ref[...] = notes[0][0:1, :].astype(jnp.int32)
 
@@ -135,59 +123,46 @@
     shift = requests.bit_length() - 1
     a = lax.broadcasted_iota(jnp.int32, (total, total), 0)
     b = lax.broadcasted_iota(jnp.int32, (total, total), 1)
-    ahead = ((lax.shift_right_logical(a, shift) == lax.shift_right_logical(b, shift)) & (a < b)).astype(bf16)
+    same_sender = lax.shift_right_logical(a, shift) == lax.shift_right_logical(b, shift)
+    ahead = (same_sender & (a < b)).astype(bf16)
     rank = jnp.dot(hit.astype(bf16), ahead, preferred_element_type=f32).astype(jnp.int32)
     lane = lax.broadcasted_iota(jnp.int32, (1, total), 1)
-    base = (s ^ lax.shift_right_logical(lane, shift)) * piece
+    base = (lax.shift_right_logical(lane, shift) ^ (s & 1)) * CAP_E
     spot = lax.broadcasted_iota(jnp.int32, (room, total), 0)
-    for chunk in range(CHUNKS):
-        for n in range(experts):
-            local = rank[n : n + 1, :] - chunk * piece
-            inside = (hit[n : n + 1, :] > 0.5) & (local >= 0) & (local < piece)
-            chosen = jnp.where(inside, base + local, -1) == spot
-            at = (chunk * experts + n) * room
-            select_ref[at : at + room, :] = jnp.where(chosen, 1.0, 0.0)
-            map_ref[at : at + room, :] = jnp.where(chosen, share[n : n + 1, :], 0.0)
+    for n in range(experts):
+        inside = (hit[n : n + 1, :] > 0.5) & (rank[n : n + 1, :] < CAP_E)
+        chosen = jnp.where(inside, base + rank[n : n + 1, :], -1) == spot
+        select_ref[n * room : (n + 1) * room, :] = jnp.where(chosen, 1.0, 0.0)
+        map_ref[n * room : (n + 1) * room, :] = jnp.where(chosen, share[n : n + 1, :], 0.0)
     select = select_ref[...].astype(bf16)
     tile = 256 if part % 256 == 0 else LANES
     for at in range(0, part, tile):
         sent = jnp.dot(select, tokens_ref[:, at : at + tile], preferred_element_type=f32)
-        for out, group in zip(outs, groups):
-            pieces = [
-                sent[(chunk * experts + n) * room : (chunk * experts + n + 1) * room, :]
-                for chunk, n in group
-            ]
-            out[:, at : at + tile] = jnp.concatenate(pieces, axis=0).astype(bf16)
+        for n in range(experts):
+            outs[n][:, at : at + tile] = sent[n * room : (n + 1) * room, :].astype(bf16)
 
 
 def dispatch(s, e, messages, part, experts, top):
-    width = len(messages)
+    senders = len(messages)
     requests = messages[0].shape[0]
-    room = width * CAP_E // CHUNKS
-    groups = message_groups(experts)
-    places = CHUNKS * experts * room
-    total = width * requests
+    room, total = senders * CAP_E, senders * requests
     *outs, weight_map, lengths = pl.pallas_call(
-        functools.partial(dispatch_kernel, width, experts, top, requests),
-        in_specs=[smem] + [vmem] * width,
-        out_specs=[vmem] * (len(groups) + 2),
-        out_shape=[jax.ShapeDtypeStruct((len(group) * room, part), bf16) for group in groups]
+        functools.partial(dispatch_kernel, senders, experts, top, requests),
+        in_specs=[smem] + [vmem] * senders,
+        out_specs=[vmem] * (experts + 2),
+        out_shape=[jax.ShapeDtypeStruct((room, part), bf16)] * experts
         + [
-            jax.ShapeDtypeStruct((places, total), f32),
+            jax.ShapeDtypeStruct((experts * room, total), f32),
             jax.ShapeDtypeStruct((1, LANES), jnp.int32),
         ],
         scratch_shapes=[
             pltpu.VMEM((total, part), bf16),
-            pltpu.VMEM((places, total), f32),
+            pltpu.VMEM((experts * room, total), f32),
         ],
         compiler_params=pltpu.CompilerParams(vmem_limit_bytes=16 * 2**20),
-        cost_estimate=pl.CostEstimate(
-            flops=2 * places * total * part,
-            bytes_accessed=2 * part * (total + places),
-            transcendentals=0,
-        ),
+        cost_estimate=little,
     )(jnp.stack([s, e]).astype(jnp.int32), *messages)
-    return outs, weight_map, lengths
+    return outs, weight_map, lengths[0, :total].reshape(senders, requests)
 
 
 def attend_all(queries, caches, lengths):
@@ -308,12 +283,15 @@
     )(where, *taken, kept)
 
 
-def total_sum(total, width):
+def total_sum(total, width, first):
     step = 2
     while step < width:
-        total = (total.astype(f32) + xor_permute(total, "steal", step).astype(f32)).astype(bf16)
+        got = xor_permute(total, "steal", step)
+        if first is not None:
+            got, first = lax.optimization_barrier((got, first))
+        total = (total.astype(f32) + got.astype(f32)).astype(bf16)
         step *= 2
-    return total
+    return total, first
 
 
 def per_device(
@@ -341,17 +319,11 @@
     messages = [messages[0]] + [xor_permute(messages[m], "steal", m) for m in range(1, width)]
     outgoing, weight_map, peer_lengths = dispatch(s, e, messages, part, experts, top)
     outgoing, peer_lengths = lax.optimization_barrier((outgoing, peer_lengths))
-    room = width * CAP_E // CHUNKS
-    pieces = {}
-    for sent, group in zip(outgoing, message_groups(experts)):
-        n = group[0][1]
-        got = sent if n == 0 else xor_permute(sent, "ep", n)
-        for at, key in enumerate(group):
-            pieces[key] = got[at * room : (at + 1) * room]
+    pieces = [outgoing[0]] + [xor_permute(outgoing[n], "ep", n) for n in range(1, experts)]
 
     slot_ids = jnp.arange(lent, dtype=jnp.int32)
     others = jnp.arange(1, width, dtype=jnp.int32)[:, None]
-    peer_lengths = peer_lengths[0, : width * requests].reshape(width, requests)[1:, :lent]
+    peer_lengths = peer_lengths[1:, :lent]
     partner = s ^ ((2 * s - steal_source[:lent]) % width)
     is_partner = partner[None, :] == others
     order = jnp.sum(jnp.where(is_partner, slot_ids[None, :], 0), axis=1)
@@ -373,10 +345,19 @@
     down_own = lax.dynamic_slice(w_down[0], (core * half, 0), (half, part))
     down_other = lax.dynamic_slice(w_down[0], ((1 - core) * half, 0), (half, part))
 
-    mixed = jnp.zeros((width * requests, part), f32)
-    for chunk in range(CHUNKS):
-        arrived = [pieces[chunk, n] for n in range(experts)]
-        arrived = jnp.concatenate(arrived, axis=0)
+    chips, chip = width // CORES, s // CORES
+    room = CORES * CAP_E
+    arrived = [
+        jnp.concatenate([pieces[n][j * room : (j + 1) * room] for n in range(experts)], axis=0)
+        for j in range(chips)
+    ]
+    by_distance = jnp.stack(arrived)
+    results = []
+    total_before, produced_before = None, None
+    for chunk in range(chips):
+        arrived = lax.dynamic_index_in_dim(by_distance, chip ^ chunk, 0, keepdims=False)
+        if chunk > 0:
+            arrived, total_before = lax.optimization_barrier((arrived, total_before))
         send = jnp.concatenate(
             [
                 jnp.dot(arrived, gate_send, preferred_element_type=f32).astype(bf16),
@@ -395,7 +376,8 @@
         total = (keep + got.astype(f32)).astype(bf16)
         if chunk == 0:
             total, taken = lax.optimization_barrier((total, taken))
-        total = total_sum(total, width)
+        total_before = total
+        total, produced_before = total_sum(total, width, produced_before)
         if chunk == 0:
             attended = place(where, taken, kept)
             total, attended = lax.optimization_barrier((total, attended))
@@ -406,23 +388,39 @@
             jnp.dot(active, down_own, preferred_element_type=f32)
             + jnp.dot(other, down_other, preferred_element_type=f32)
         ).astype(bf16)
-        produced = produced.reshape(experts, room, part)
-        returned = jnp.concatenate(
-            [produced[0]] + [xor_permute(produced[n], "ep", n) for n in range(1, experts)],
-            axis=0,
-        )
-        mixed = mixed + jnp.einsum(
+        produced_before = produced
+        results.append(produced.reshape(experts, room, part))
+
+    results = jnp.stack(results)
+    back = [lax.dynamic_index_in_dim(results, chip ^ j, 0, keepdims=False) for j in range(chips)]
+    far = jnp.concatenate(back[1:], axis=1)
+    near = back[0]
+    far_rows = far.shape[1]
+    both = xor_permute(jnp.concatenate([far[1], near[1]], axis=0), "ep", 1)
+    far = [far[0], both[:far_rows]] + [xor_permute(far[n], "ep", n) for n in range(2, experts)]
+    near = [near[0], both[far_rows:]] + [xor_permute(near[n], "ep", n) for n in range(2, experts)]
+
+    def mix(weight_map, returned):
+        returned = jnp.concatenate(returned, axis=0).astype(f32)
+        mixed = jnp.einsum(
             "ir,ik->rk",
-            weight_map[chunk * experts * room : (chunk + 1) * experts * room],
-            returned.astype(f32),
+            weight_map,
+            returned,
             precision=lax.Precision.HIGHEST,
             preferred_element_type=f32,
         )
-    mixed = mixed.astype(bf16).reshape(width, requests, part)
+        return mixed.astype(bf16).reshape(-1, requests, part)
+
+    weight_map = weight_map.reshape(experts, width * CAP_E, width * requests)
+    split = CORES * requests
+    mixed = mix(weight_map[:, room:, split:].reshape(-1, width * requests - split), far)
+    got = [xor_permute(mixed[m - CORES], "steal", m) for m in range(CORES, width)]
+    near, got = lax.optimization_barrier((near, got))
+    mixed = mix(weight_map[:, :room, :split].reshape(-1, split), near)
+    got = [mixed[0], xor_permute(mixed[1], "steal", 1)] + got
     result = jnp.zeros((requests, model_width), bf16)
     for m in range(width):
-        got = mixed[m] if m == 0 else xor_permute(mixed[m], "steal", m)
-        result = lax.dynamic_update_slice(result, got, (0, (s ^ m) * part))
+        result = lax.dynamic_update_slice(result, got[m], (0, (s ^ m) * part))
     return (attended, result)
 
 

time: 73.1 us -> 71.8 us (0.982)
  the two profiles are of different devices: /device:TPU:0 before, /device:TPU:17 now
where the time goes in v3:
time: 71.8 us; the launch traced here: 71.5 us
  starting transfers between devices  24.4 us (34%)
  waiting for transfers between devices  24.4 us (34%)
  Pallas kernels  8.64 us (12%)
  matrix products  5.91 us (8%)
  local copies, waits for them, and re-layouts  5.23 us (7%)
  other arithmetic  1.92 us (3%)
  between operations  0.97 us (1%)
    ppermute x23, starting transfers between devices, xor_permute(): return lax.ppermute(x, axis, [(i, i ^ m) for i in range(size)])  24.4 us
    ppermute x23, waiting for transfers between devices, xor_permute(): return lax.ppermute(x, axis, [(i, i ^ m) for i in range(size)])  24.4 us
    unnamed x18, local copies, waits for them, and re-layouts  4.86 us
    pallas_call x1, Pallas kernels, attend_kept(): pl.pallas_call(functools.partial(kept_kernel, step), grid_spec=pltpu.Pref...  3.27 us
    pallas_call x1, Pallas kernels, prepare(): pl.pallas_call(functools.partial(prepare_kernel, width), in_specs=[smem]...  1.9 us
  transfers between devices with their start and end apart: 23, of which 13 were waited for; matrix products, arithmetic and copies ran while one was open for 8% of the time, Pallas kernels for 8%

profile of v3, /device:TPU:17, one launch (start us, length us, event | category | flops | bytes accessed | tf_op | source)
XLA Modules:
  0.0 71.5 jit_solution(16729020486299644283)
XLA Ops:
  0.6 1.9 %shard_map.122 = (bf16[16,1920]{1,0:T(8,128)(2,1)}, bf16[16,1920]{1,0:T(8,128)(2,1)}, bf16[16,1920]{1,0:T(8,128)(2,1)}, bf16[16,1920]{1,0:T(8,128)(2,1)}) custom-call(s32[1]{0:T(128)} %bitcast.here_ref, bf16[16,7168]{1,0:T(8,128)(2,1)} %hidden_ref.1, f32[1,7168]{1,0:T(1,128)} %bitcast.103, s32[1,16]{1,0:T(1,128)} %bitcast.98, s32[2,16]{1,0:T(2,128)} %bitcast.104, ...), custom_call_target="tpu_custom_call" | custom-call | tf_op jit(solution)/shard_map/pallas_call | solution.py:72
  3.2 1.2 %collective-permute-start.1 = (bf16[16,1920]{1,0:T(8,128)(2,1)}, bf16[16,1920]{1,0:T(8,128)(2,1)S(1)}, u32[]{:S(2)}, u32[]{:S(2)}) collective-permute-start(bf16[16,1920]{1,0:T(8,128)(2,1)} %get-tuple-element.45), channel_id=1, source_target_pairs={{0,8},{4,12},{8,0},{12,4},{1,9},{5,13},{9,1},{13,5},{2,10},{6,14},... | collective-permute-start | bytes 184328 | tf_op jit(solution)/shard_map/ppermute | solution.py:30
  5.6 1.4 %collective-permute-done.1.refs_2_ = bf16[16,1920]{1,0:T(8,128)(2,1)S(1)} collective-permute-done((bf16[16,1920]{1,0:T(8,128)(2,1)}, bf16[16,1920]{1,0:T(8,128)(2,1)S(1)}, u32[]{:S(2)}, u32[]{:S(2)}) %collective-permute-start.1) | collective-permute-done | bytes 61472 | tf_op jit(solution)/shard_map/ppermute | solution.py:30
  7.0 1.5 %collective-permute-done.2.refs_3_ = bf16[16,1920]{1,0:T(8,128)(2,1)S(1)} collective-permute-done((bf16[16,1920]{1,0:T(8,128)(2,1)}, bf16[16,1920]{1,0:T(8,128)(2,1)S(1)}, u32[]{:S(2)}, u32[]{:S(2)}) %collective-permute-start.2) | collective-permute-done | bytes 61472 | tf_op jit(solution)/shard_map/ppermute | solution.py:30
  10.5 1.3 %collective-permute-start.3 = (bf16[48,1792]{1,0:T(8,128)(2,1)S(1)}, bf16[48,1792]{1,0:T(8,128)(2,1)S(1)}, u32[]{:S(2)}, u32[]{:S(2)}) collective-permute-start(bf16[48,1792]{1,0:T(8,128)(2,1)S(1)} %get-tuple-element.53), channel_id=1, source_target_pairs={{0,1},{1,0},{2,3},{3,2},{4,5},{5,4},{6,7},{7,6},{8,9},{9,8},{10,11... | collective-permute-start | bytes 516104 | tf_op jit(solution)/shard_map/ppermute | solution.py:30
  11.9 1.3 %collective-permute-start.5 = (bf16[48,1792]{1,0:T(8,128)(2,1)S(1)}, bf16[48,1792]{1,0:T(8,128)(2,1)S(1)}, u32[]{:S(2)}, u32[]{:S(2)}) collective-permute-start(bf16[48,1792]{1,0:T(8,128)(2,1)S(1)} %get-tuple-element.55), channel_id=1, source_target_pairs={{0,3},{1,2},{2,1},{3,0},{4,7},{5,6},{6,5},{7,4},{8,11},{9,10},{10,... | collective-permute-start | bytes 516104 | tf_op jit(solution)/shard_map/ppermute | solution.py:30
  13.4 1.7 %copy-done = bf16[16,128,576]{1,2,0:T(8,128)(2,1)S(1)} copy-done((bf16[16,128,576]{1,2,0:T(8,128)(2,1)S(1)}, bf16[16,128,576]{1,2,0:T(8,128)(2,1)}, u32[]{:S(2)}) %copy-start) | copy-done | bytes 2359320
  15.0 1.7 %copy-done.2 = bf16[16,128,576]{1,2,0:T(8,128)(2,1)S(1)} copy-done((bf16[16,128,576]{1,2,0:T(8,128)(2,1)S(1)}, bf16[16,128,576]{1,2,0:T(8,128)(2,1)}, u32[]{:S(2)}) %copy-start.2) | copy-done | bytes 2359320
  17.9 1.3 %collective-permute-start.7 = (bf16[128,512]{1,0:T(8,128)(2,1)S(1)}, bf16[128,512]{1,0:T(8,128)(2,1)S(1)}, u32[]{:S(2)}, u32[]{:S(2)}) collective-permute-start(bf16[128,512]{1,0:T(8,128)(2,1)S(1)} %get-tuple-element.65), channel_id=1, source_target_pairs={{0,4},{4,0},{8,12},{12,8},{1,5},{5,1},{9,13},{13,9},{2,6},{6,2},{1... | collective-permute-start | bytes 393224 | tf_op jit(solution)/shard_map/ppermute | solution.py:30
  20.2 3.3 %shard_map.125.refs_3_ = bf16[16,128,512]{2,1,0:T(8,128)(2,1)} custom-call(s32[16]{0:T(128)S(1)} %copy-done.4, bf16[16,576,128]{2,1,0:T(8,128)(2,1)S(1)} %bitcast.92, bf16[16,576,128]{2,1,0:T(8,128)(2,1)S(1)} %bitcast.96), custom_call_target="tpu_custom_call" | custom-call | flops 570425344 | bytes 6815744 | tf_op jit(solution)/shard_map/pallas_call | solution.py:212
  24.2 3.9 %collective-permute-done.5 = bf16[48,1792]{1,0:T(8,128)(2,1)S(1)} collective-permute-done((bf16[48,1792]{1,0:T(8,128)(2,1)S(1)}, bf16[48,1792]{1,0:T(8,128)(2,1)S(1)}, u32[]{:S(2)}, u32[]{:S(2)}) %collective-permute-start.5) | collective-permute-done | bytes 172064 | tf_op jit(solution)/shard_map/ppermute | solution.py:30
  29.4 1.6 %collective-permute-start.6 = (bf16[96,1024]{1,0:T(8,128)(2,1)S(1)}, bf16[96,1024]{1,0:T(8,128)(2,1)S(1)}, u32[]{:S(2)}, u32[]{:S(2)}) collective-permute-start(bf16[96,1024]{1,0:T(8,128)(2,1)S(1)} %pad_maximum_fusion), channel_id=1, source_target_pairs={{0,4},{4,0},{8,12},{12,8},{1,5},{5,1},{9,13},{13,9},{2,6},{6,2},{1... | collective-permute-start | bytes 589832 | tf_op jit(solution)/shard_map/ppermute | solution.py:30
  33.5 1.2 %collective-permute-start.10 = (bf16[96,1024]{1,0:T(8,128)(2,1)S(1)}, bf16[96,1024]{1,0:T(8,128)(2,1)S(1)}, u32[]{:S(2)}, u32[]{:S(2)}) collective-permute-start(bf16[96,1024]{1,0:T(8,128)(2,1)S(1)} %fusion.48), channel_id=1, source_target_pairs={{0,8},{4,12},{8,0},{12,4},{1,9},{5,13},{9,1},{13,5},{2,10},{6,14},... | collective-permute-start | bytes 589832 | tf_op jit(solution)/shard_map/ppermute | solution.py:30
  35.4 1.3 %shard_map.126 = bf16[16,128,512]{2,1,0:T(8,128)(2,1)} custom-call(s32[3]{0:T(128)S(1)} %get-tuple-element.86.where_ref, bf16[128,512]{1,0:T(8,128)(2,1)S(1)} %collective-permute-done.7.refs_0_, bf16[128,512]{1,0:T(8,128)(2,1)S(1)} %collective-permute-done.8.refs_1_, ...), custom_call_target="tpu_custom_call", output_to_operand_aliasing={{}: (4, {})} | custom-call | tf_op jit(solution)/shard_map/pallas_call | solution.py:275
  37.7 2.0 %collective-permute-done.10 = bf16[96,1024]{1,0:T(8,128)(2,1)S(1)} collective-permute-done((bf16[96,1024]{1,0:T(8,128)(2,1)S(1)}, bf16[96,1024]{1,0:T(8,128)(2,1)S(1)}, u32[]{:S(2)}, u32[]{:S(2)}) %collective-permute-start.10) | collective-permute-done | bytes 196640 | tf_op jit(solution)/shard_map/ppermute | solution.py:30
  39.8 1.7 %collective-permute-start.11 = (bf16[96,512]{1,0:T(8,128)(2,1)S(1)}, bf16[96,512]{1,0:T(8,128)(2,1)S(1)}, u32[]{:S(2)}, u32[]{:S(2)}) collective-permute-start(bf16[96,512]{1,0:T(8,128)(2,1)S(1)} %fusion.72), channel_id=1, source_target_pairs={{0,4},{4,0},{8,12},{12,8},{1,5},{5,1},{9,13},{13,9},{2,6},{6,2},{1... | collective-permute-start | bytes 294920 | tf_op jit(solution)/shard_map/ppermute | solution.py:30
  42.8 1.5 %collective-permute-done.13 = bf16[96,1024]{1,0:T(8,128)(2,1)S(1)} collective-permute-done((bf16[96,1024]{1,0:T(8,128)(2,1)S(1)}, bf16[96,1024]{1,0:T(8,128)(2,1)S(1)}, u32[]{:S(2)}, u32[]{:S(2)}) %collective-permute-start.13) | collective-permute-done | bytes 196640 | tf_op jit(solution)/shard_map/ppermute | solution.py:30
  47.2 1.3 %collective-permute-start.18 = (bf16[24,1792]{1,0:T(8,128)(2,1)S(1)}, bf16[24,1792]{1,0:T(8,128)(2,1)S(1)}, u32[]{:S(2)}, u32[]{:S(2)}) collective-permute-start(bf16[24,1792]{1,0:T(8,128)(2,1)S(1)} %get-tuple-element.92), channel_id=1, source_target_pairs={{0,2},{1,3},{2,0},{3,1},{4,6},{5,7},{6,4},{7,5},{8,10},{9,11},{10,... | collective-permute-start | bytes 258056 | tf_op jit(solution)/shard_map/ppermute | solution.py:30
  48.5 1.3 %collective-permute-start.19 = (bf16[24,1792]{1,0:T(8,128)(2,1)S(1)}, bf16[24,1792]{1,0:T(8,128)(2,1)S(1)}, u32[]{:S(2)}, u32[]{:S(2)}) collective-permute-start(bf16[24,1792]{1,0:T(8,128)(2,1)S(1)} %get-tuple-element.94), channel_id=1, source_target_pairs={{0,3},{1,2},{2,1},{3,0},{4,7},{5,6},{6,5},{7,4},{8,11},{9,10},{10,... | collective-permute-start | bytes 258056 | tf_op jit(solution)/shard_map/ppermute | solution.py:30
  52.7 1.7 %collective-permute-done.18 = bf16[24,1792]{1,0:T(8,128)(2,1)S(1)} collective-permute-done((bf16[24,1792]{1,0:T(8,128)(2,1)S(1)}, bf16[24,1792]{1,0:T(8,128)(2,1)S(1)}, u32[]{:S(2)}, u32[]{:S(2)}) %collective-permute-start.18) | collective-permute-done | bytes 86048 | tf_op jit(solution)/shard_map/ppermute | solution.py:30
  54.4 6.3 %collective-permute-done.19 = bf16[24,1792]{1,0:T(8,128)(2,1)S(1)} collective-permute-done((bf16[24,1792]{1,0:T(8,128)(2,1)S(1)}, bf16[24,1792]{1,0:T(8,128)(2,1)S(1)}, u32[]{:S(2)}, u32[]{:S(2)}) %collective-permute-start.19) | collective-permute-done | bytes 86048 | tf_op jit(solution)/shard_map/ppermute | solution.py:30
  61.1 1.2 %collective-permute-start.20 = (bf16[16,1792]{1,0:T(8,128)(2,1)S(1)}, bf16[16,1792]{1,0:T(8,128)(2,1)S(1)}, u32[]{:S(2)}, u32[]{:S(2)}) collective-permute-start(bf16[16,1792]{1,0:T(8,128)(2,1)S(1)} %get-tuple-element.112), channel_id=1, source_target_pairs={{0,8},{4,12},{8,0},{12,4},{1,9},{5,13},{9,1},{13,5},{2,10},{6,14},... | collective-permute-start | bytes 172040 | tf_op jit(solution)/shard_map/ppermute | solution.py:30
  62.2 3.4 %collective-permute-start.21 = (bf16[16,1792]{1,0:T(8,128)(2,1)S(1)}, bf16[16,1792]{1,0:T(8,128)(2,1)S(1)}, u32[]{:S(2)}, u32[]{:S(2)}) collective-permute-start(bf16[16,1792]{1,0:T(8,128)(2,1)S(1)} %get-tuple-element.111), channel_id=1, source_target_pairs={{0,12},{4,8},{8,4},{12,0},{1,13},{5,9},{9,5},{13,1},{2,14},{6,10},... | collective-permute-start | bytes 172040 | tf_op jit(solution)/shard_map/ppermute | solution.py:30
  65.7 3.2 %collective-permute-done.21 = bf16[16,1792]{1,0:T(8,128)(2,1)S(1)} collective-permute-done((bf16[16,1792]{1,0:T(8,128)(2,1)S(1)}, bf16[16,1792]{1,0:T(8,128)(2,1)S(1)}, u32[]{:S(2)}, u32[]{:S(2)}) %collective-permute-start.21) | collective-permute-done | bytes 57376 | tf_op jit(solution)/shard_map/ppermute | solution.py:30
  (92 shorter events, 22.5 us)
Async XLA Ops:
  2.5 3.1 %collective-permute-start = (bf16[16,1920]{1,0:T(8,128)(2,1)}, bf16[16,1920]{1,0:T(8,128)(2,1)S(1)}, u32[]{:S(2)}, u32[]{:S(2)}) collective-permute-start(bf16[16,1920]{1,0:T(8,128)(2,1)} %get-tuple-element.44), channel_id=1, source_target_pairs={{0,4},{4,0},{8,12},{12,8},{1,5},{5,1},{9,13},{13,9},{2,6},{6,2},{1... | collective-permute-start | bytes 184328 | tf_op jit(solution)/shard_map/ppermute | solution.py:30
  3.2 3.8 %collective-permute-start.1 = (bf16[16,1920]{1,0:T(8,128)(2,1)}, bf16[16,1920]{1,0:T(8,128)(2,1)S(1)}, u32[]{:S(2)}, u32[]{:S(2)}) collective-permute-start(bf16[16,1920]{1,0:T(8,128)(2,1)} %get-tuple-element.45), channel_id=1, source_target_pairs={{0,8},{4,12},{8,0},{12,4},{1,9},{5,13},{9,1},{13,5},{2,10},{6,14},... | collective-permute-start | bytes 184328 | tf_op jit(solution)/shard_map/ppermute | solution.py:30
  4.4 4.1 %collective-permute-start.2 = (bf16[16,1920]{1,0:T(8,128)(2,1)}, bf16[16,1920]{1,0:T(8,128)(2,1)S(1)}, u32[]{:S(2)}, u32[]{:S(2)}) collective-permute-start(bf16[16,1920]{1,0:T(8,128)(2,1)} %get-tuple-element.46), channel_id=1, source_target_pairs={{0,12},{4,8},{8,4},{12,0},{1,13},{5,9},{9,5},{13,1},{2,14},{6,10},... | collective-permute-start | bytes 184328 | tf_op jit(solution)/shard_map/ppermute | solution.py:30
  10.5 13.0 %collective-permute-start.3 = (bf16[48,1792]{1,0:T(8,128)(2,1)S(1)}, bf16[48,1792]{1,0:T(8,128)(2,1)S(1)}, u32[]{:S(2)}, u32[]{:S(2)}) collective-permute-start(bf16[48,1792]{1,0:T(8,128)(2,1)S(1)} %get-tuple-element.53), channel_id=1, source_target_pairs={{0,1},{1,0},{2,3},{3,2},{4,5},{5,4},{6,7},{7,6},{8,9},{9,8},{10,11... | collective-permute-start | bytes 516104 | tf_op jit(solution)/shard_map/ppermute | solution.py:30
  11.8 12.4 %collective-permute-start.4 = (bf16[48,1792]{1,0:T(8,128)(2,1)S(1)}, bf16[48,1792]{1,0:T(8,128)(2,1)S(1)}, u32[]{:S(2)}, u32[]{:S(2)}) collective-permute-start(bf16[48,1792]{1,0:T(8,128)(2,1)S(1)} %get-tuple-element.54), channel_id=1, source_target_pairs={{0,2},{1,3},{2,0},{3,1},{4,6},{5,7},{6,4},{7,5},{8,10},{9,11},{10,... | collective-permute-start | bytes 516104 | tf_op jit(solution)/shard_map/ppermute | solution.py:30
  11.9 16.2 %collective-permute-start.5 = (bf16[48,1792]{1,0:T(8,128)(2,1)S(1)}, bf16[48,1792]{1,0:T(8,128)(2,1)S(1)}, u32[]{:S(2)}, u32[]{:S(2)}) collective-permute-start(bf16[48,1792]{1,0:T(8,128)(2,1)S(1)} %get-tuple-element.55), channel_id=1, source_target_pairs={{0,3},{1,2},{2,1},{3,0},{4,7},{5,6},{6,5},{7,4},{8,11},{9,10},{10,... | collective-permute-start | bytes 516104 | tf_op jit(solution)/shard_map/ppermute | solution.py:30
  17.9 14.3 %collective-permute-start.7 = (bf16[128,512]{1,0:T(8,128)(2,1)S(1)}, bf16[128,512]{1,0:T(8,128)(2,1)S(1)}, u32[]{:S(2)}, u32[]{:S(2)}) collective-permute-start(bf16[128,512]{1,0:T(8,128)(2,1)S(1)} %get-tuple-element.65), channel_id=1, source_target_pairs={{0,4},{4,0},{8,12},{12,8},{1,5},{5,1},{9,13},{13,9},{2,6},{6,2},{1... | collective-permute-start | bytes 393224 | tf_op jit(solution)/shard_map/ppermute | solution.py:30
  19.2 13.0 %collective-permute-start.8 = (bf16[128,512]{1,0:T(8,128)(2,1)S(1)}, bf16[128,512]{1,0:T(8,128)(2,1)S(1)}, u32[]{:S(2)}, u32[]{:S(2)}) collective-permute-start(bf16[128,512]{1,0:T(8,128)(2,1)S(1)} %get-tuple-element.66), channel_id=1, source_target_pairs={{0,8},{4,12},{8,0},{12,4},{1,9},{5,13},{9,1},{13,5},{2,10},{6,14},... | collective-permute-start | bytes 393224 | tf_op jit(solution)/shard_map/ppermute | solution.py:30
  20.2 8.8 %copy-start.6 = (bf16[1,1792,1024]{2,1,0:T(8,128)(2,1)S(1)}, bf16[1,1792,1024]{2,1,0:T(8,128)(2,1)}, u32[]{:S(2)}) copy-start(bf16[1,1792,1024]{2,1,0:T(8,128)(2,1)} %param.20) | copy-start | bytes 11010052
  23.5 8.7 %collective-permute-start.9 = (bf16[128,512]{1,0:T(8,128)(2,1)S(1)}, bf16[128,512]{1,0:T(8,128)(2,1)S(1)}, u32[]{:S(2)}, u32[]{:S(2)}) collective-permute-start(bf16[128,512]{1,0:T(8,128)(2,1)S(1)} %get-tuple-element.67), channel_id=1, source_target_pairs={{0,12},{4,8},{8,4},{12,0},{1,13},{5,9},{9,5},{13,1},{2,14},{6,10},... | collective-permute-start | bytes 393224 | tf_op jit(solution)/shard_map/ppermute | solution.py:30
  29.4 2.7 %collective-permute-start.6 = (bf16[96,1024]{1,0:T(8,128)(2,1)S(1)}, bf16[96,1024]{1,0:T(8,128)(2,1)S(1)}, u32[]{:S(2)}, u32[]{:S(2)}) collective-permute-start(bf16[96,1024]{1,0:T(8,128)(2,1)S(1)} %pad_maximum_fusion), channel_id=1, source_target_pairs={{0,4},{4,0},{8,12},{12,8},{1,5},{5,1},{9,13},{13,9},{2,6},{6,2},{1... | collective-permute-start | bytes 589832 | tf_op jit(solution)/shard_map/ppermute | solution.py:30
  33.5 6.2 %collective-permute-start.10 = (bf16[96,1024]{1,0:T(8,128)(2,1)S(1)}, bf16[96,1024]{1,0:T(8,128)(2,1)S(1)}, u32[]{:S(2)}, u32[]{:S(2)}) collective-permute-start(bf16[96,1024]{1,0:T(8,128)(2,1)S(1)} %fusion.48), channel_id=1, source_target_pairs={{0,8},{4,12},{8,0},{12,4},{1,9},{5,13},{9,1},{13,5},{2,10},{6,14},... | collective-permute-start | bytes 589832 | tf_op jit(solution)/shard_map/ppermute | solution.py:30
  34.7 2.5 %collective-permute-start.12 = (bf16[96,1024]{1,0:T(8,128)(2,1)S(1)}, bf16[96,1024]{1,0:T(8,128)(2,1)S(1)}, u32[]{:S(2)}, u32[]{:S(2)}) collective-permute-start(bf16[96,1024]{1,0:T(8,128)(2,1)S(1)} %pad_maximum_fusion.1), channel_id=1, source_target_pairs={{0,4},{4,0},{8,12},{12,8},{1,5},{5,1},{9,13},{13,9},{2,6},{6,2},{1... | collective-permute-start | bytes 589832 | tf_op jit(solution)/shard_map/ppermute | solution.py:30
  37.3 7.1 %collective-permute-start.13 = (bf16[96,1024]{1,0:T(8,128)(2,1)S(1)}, bf16[96,1024]{1,0:T(8,128)(2,1)S(1)}, u32[]{:S(2)}, u32[]{:S(2)}) collective-permute-start(bf16[96,1024]{1,0:T(8,128)(2,1)S(1)} %fusion.49), channel_id=1, source_target_pairs={{0,8},{4,12},{8,0},{12,4},{1,9},{5,13},{9,1},{13,5},{2,10},{6,14},... | collective-permute-start | bytes 589832 | tf_op jit(solution)/shard_map/ppermute | solution.py:30
  39.8 2.6 %collective-permute-start.11 = (bf16[96,512]{1,0:T(8,128)(2,1)S(1)}, bf16[96,512]{1,0:T(8,128)(2,1)S(1)}, u32[]{:S(2)}, u32[]{:S(2)}) collective-permute-start(bf16[96,512]{1,0:T(8,128)(2,1)S(1)} %fusion.72), channel_id=1, source_target_pairs={{0,4},{4,0},{8,12},{12,8},{1,5},{5,1},{9,13},{13,9},{2,6},{6,2},{1... | collective-permute-start | bytes 294920 | tf_op jit(solution)/shard_map/ppermute | solution.py:30
  44.4 1.8 %collective-permute-start.14 = (bf16[96,512]{1,0:T(8,128)(2,1)S(1)}, bf16[96,512]{1,0:T(8,128)(2,1)S(1)}, u32[]{:S(2)}, u32[]{:S(2)}) collective-permute-start(bf16[96,512]{1,0:T(8,128)(2,1)S(1)} %fusion.71), channel_id=1, source_target_pairs={{0,4},{4,0},{8,12},{12,8},{1,5},{5,1},{9,13},{13,9},{2,6},{6,2},{1... | collective-permute-start | bytes 294920 | tf_op jit(solution)/shard_map/ppermute | solution.py:30
  47.0 5.7 %collective-permute-start.15 = (bf16[48,1792]{1,0:T(8,128)(2,1)S(1)}, bf16[48,1792]{1,0:T(8,128)(2,1)S(1)}, u32[]{:S(2)}, u32[]{:S(2)}) collective-permute-start(bf16[48,1792]{1,0:T(8,128)(2,1)S(1)} %pad_maximum_fusion.2), channel_id=1, source_target_pairs={{0,1},{1,0},{2,3},{3,2},{4,5},{5,4},{6,7},{7,6},{8,9},{9,8},{10,11... | collective-permute-start | bytes 516104 | tf_op jit(solution)/shard_map/ppermute | solution.py:30
  47.2 7.2 %collective-permute-start.18 = (bf16[24,1792]{1,0:T(8,128)(2,1)S(1)}, bf16[24,1792]{1,0:T(8,128)(2,1)S(1)}, u32[]{:S(2)}, u32[]{:S(2)}) collective-permute-start(bf16[24,1792]{1,0:T(8,128)(2,1)S(1)} %get-tuple-element.92), channel_id=1, source_target_pairs={{0,2},{1,3},{2,0},{3,1},{4,6},{5,7},{6,4},{7,5},{8,10},{9,11},{10,... | collective-permute-start | bytes 258056 | tf_op jit(solution)/shard_map/ppermute | solution.py:30
  48.5 12.2 %collective-permute-start.19 = (bf16[24,1792]{1,0:T(8,128)(2,1)S(1)}, bf16[24,1792]{1,0:T(8,128)(2,1)S(1)}, u32[]{:S(2)}, u32[]{:S(2)}) collective-permute-start(bf16[24,1792]{1,0:T(8,128)(2,1)S(1)} %get-tuple-element.94), channel_id=1, source_target_pairs={{0,3},{1,2},{2,1},{3,0},{4,7},{5,6},{6,5},{7,4},{8,11},{9,10},{10,... | collective-permute-start | bytes 258056 | tf_op jit(solution)/shard_map/ppermute | solution.py:30
  49.8 15.9 %collective-permute-start.16 = (bf16[24,1792]{1,0:T(8,128)(2,1)S(1)}, bf16[24,1792]{1,0:T(8,128)(2,1)S(1)}, u32[]{:S(2)}, u32[]{:S(2)}) collective-permute-start(bf16[24,1792]{1,0:T(8,128)(2,1)S(1)} %get-tuple-element.96), channel_id=1, source_target_pairs={{0,2},{1,3},{2,0},{3,1},{4,6},{5,7},{6,4},{7,5},{8,10},{9,11},{10,... | collective-permute-start | bytes 258056 | tf_op jit(solution)/shard_map/ppermute | solution.py:30
  50.8 14.9 %collective-permute-start.17 = (bf16[24,1792]{1,0:T(8,128)(2,1)S(1)}, bf16[24,1792]{1,0:T(8,128)(2,1)S(1)}, u32[]{:S(2)}, u32[]{:S(2)}) collective-permute-start(bf16[24,1792]{1,0:T(8,128)(2,1)S(1)} %get-tuple-element.95), channel_id=1, source_target_pairs={{0,3},{1,2},{2,1},{3,0},{4,7},{5,6},{6,5},{7,4},{8,11},{9,10},{10,... | collective-permute-start | bytes 258056 | tf_op jit(solution)/shard_map/ppermute | solution.py:30
  61.1 4.6 %collective-permute-start.20 = (bf16[16,1792]{1,0:T(8,128)(2,1)S(1)}, bf16[16,1792]{1,0:T(8,128)(2,1)S(1)}, u32[]{:S(2)}, u32[]{:S(2)}) collective-permute-start(bf16[16,1792]{1,0:T(8,128)(2,1)S(1)} %get-tuple-element.112), channel_id=1, source_target_pairs={{0,8},{4,12},{8,0},{12,4},{1,9},{5,13},{9,1},{13,5},{2,10},{6,14},... | collective-permute-start | bytes 172040 | tf_op jit(solution)/shard_map/ppermute | solution.py:30
  62.2 6.6 %collective-permute-start.21 = (bf16[16,1792]{1,0:T(8,128)(2,1)S(1)}, bf16[16,1792]{1,0:T(8,128)(2,1)S(1)}, u32[]{:S(2)}, u32[]{:S(2)}) collective-permute-start(bf16[16,1792]{1,0:T(8,128)(2,1)S(1)} %get-tuple-element.111), channel_id=1, source_target_pairs={{0,12},{4,8},{8,4},{12,0},{1,13},{5,9},{9,5},{13,1},{2,14},{6,10},... | collective-permute-start | bytes 172040 | tf_op jit(solution)/shard_map/ppermute | solution.py:30
  69.2 1.5 %collective-permute-start.22 = (bf16[16,1792]{1,0:T(8,128)(2,1)S(1)}, bf16[16,1792]{1,0:T(8,128)(2,1)S(1)}, u32[]{:S(2)}, u32[]{:S(2)}) collective-permute-start(bf16[16,1792]{1,0:T(8,128)(2,1)S(1)} %get-tuple-element.109), channel_id=1, source_target_pairs={{0,4},{4,0},{8,12},{12,8},{1,5},{5,1},{9,13},{13,9},{2,6},{6,2},{1... | collective-permute-start | bytes 172040 | tf_op jit(solution)/shard_map/ppermute | solution.py:30
  (8 other events, 21.6 us)

commit v4 on v3

--- a/solution.py
+++ b/solution.py
@@ -165,6 +165,21 @@
     return outs, weight_map, lengths[0, :total].reshape(senders, requests)
 
 
+def hold_kernel(in_ref, out_ref):
+    out_ref[...] = in_ref[...]
+
+
+def hold(x):
+    return pl.pallas_call(
+        hold_kernel,
+        in_specs=[vmem],
+        out_specs=vmem,
+        out_shape=jax.ShapeDtypeStruct(x.shape, x.dtype),
+        compiler_params=pltpu.CompilerParams(vmem_limit_bytes=2 * 2**20),
+        cost_estimate=little,
+    )(x)
+
+
 def attend_all(queries, caches, lengths):
     scores = [
         lax.dot_general(cache, query, (((0,), (0,)), ((), ())), preferred_element_type=f32)
@@ -316,7 +331,7 @@
     lent = width - 1
 
     messages = prepare(s, hidden, norm_gain, cache_length, expert_ids, expert_weight, width)
-    messages = [messages[0]] + [xor_permute(messages[m], "steal", m) for m in range(1, width)]
+    messages = [hold(messages[0])] + [xor_permute(messages[m], "steal", m) for m in range(1, width)]
     outgoing, weight_map, peer_lengths = dispatch(s, e, messages, part, experts, top)
     outgoing, peer_lengths = lax.optimization_barrier((outgoing, peer_lengths))
     pieces = [outgoing[0]] + [xor_permute(outgoing[n], "ep", n) for n in range(1, experts)]

time: 71.8 us -> 70.9 us (0.987)
  waiting for transfers between devices: 24.4 us -> 23.6 us
    ppermute x23, waiting for transfers between devices: 24.4 us -> 23.6 us  [xor_permute(): return lax.ppermute(x, axis, [(i, i ^ m) for i in range(size)])]
where the time goes in v4:
time: 70.9 us; the launch traced here: 70.7 us
  starting transfers between devices  24.5 us (35%)
  waiting for transfers between devices  23.6 us (33%)
  Pallas kernels  8.64 us (12%)
  matrix products  5.91 us (8%)
  local copies, waits for them, and re-layouts  5.23 us (7%)
  other arithmetic  1.92 us (3%)
  between operations  0.98 us (1%)
    ppermute x23, starting transfers between devices, xor_permute(): return lax.ppermute(x, axis, [(i, i ^ m) for i in range(size)])  24.5 us
    ppermute x23, waiting for transfers between devices, xor_permute(): return lax.ppermute(x, axis, [(i, i ^ m) for i in range(size)])  23.6 us
    unnamed x18, local copies, waits for them, and re-layouts  4.86 us
    pallas_call x1, Pallas kernels, attend_kept(): pl.pallas_call(functools.partial(kept_kernel, step), grid_spec=pltpu.Pref...  3.27 us
    pallas_call x1, Pallas kernels, prepare(): pl.pallas_call(functools.partial(prepare_kernel, width), in_specs=[smem]...  1.9 us
  transfers between devices with their start and end apart: 23, of which 13 were waited for; matrix products, arithmetic and copies ran while one was open for 8% of the time, Pallas kernels for 8%

profile of v4, /device:TPU:17, one launch (start us, length us, event | category | flops | bytes accessed | tf_op | source)
XLA Modules:
  0.0 70.7 jit_solution(13770741179446934884)
XLA Ops:
  0.6 1.9 %shard_map.122 = (bf16[16,1920]{1,0:T(8,128)(2,1)}, bf16[16,1920]{1,0:T(8,128)(2,1)}, bf16[16,1920]{1,0:T(8,128)(2,1)}, bf16[16,1920]{1,0:T(8,128)(2,1)}) custom-call(s32[1]{0:T(128)} %bitcast.here_ref, bf16[16,7168]{1,0:T(8,128)(2,1)} %hidden_ref.1, f32[1,7168]{1,0:T(1,128)} %bitcast.103, s32[1,16]{1,0:T(1,128)} %bitcast.98, s32[2,16]{1,0:T(2,128)} %bitcast.104, ...), custom_call_target="tpu_custom_call" | custom-call | tf_op jit(solution)/shard_map/pallas_call | solution.py:72
  3.2 1.2 %collective-permute-start.1 = (bf16[16,1920]{1,0:T(8,128)(2,1)}, bf16[16,1920]{1,0:T(8,128)(2,1)S(1)}, u32[]{:S(2)}, u32[]{:S(2)}) collective-permute-start(bf16[16,1920]{1,0:T(8,128)(2,1)} %get-tuple-element.45), channel_id=1, source_target_pairs={{0,8},{4,12},{8,0},{12,4},{1,9},{5,13},{9,1},{13,5},{2,10},{6,14},... | collective-permute-start | bytes 184328 | tf_op jit(solution)/shard_map/ppermute | solution.py:30
  7.0 1.5 %collective-permute-done.2.refs_3_ = bf16[16,1920]{1,0:T(8,128)(2,1)S(1)} collective-permute-done((bf16[16,1920]{1,0:T(8,128)(2,1)}, bf16[16,1920]{1,0:T(8,128)(2,1)S(1)}, u32[]{:S(2)}, u32[]{:S(2)}) %collective-permute-start.2) | collective-permute-done | bytes 61472 | tf_op jit(solution)/shard_map/ppermute | solution.py:30
  9.7 1.3 %collective-permute-start.3 = (bf16[48,1792]{1,0:T(8,128)(2,1)S(1)}, bf16[48,1792]{1,0:T(8,128)(2,1)S(1)}, u32[]{:S(2)}, u32[]{:S(2)}) collective-permute-start(bf16[48,1792]{1,0:T(8,128)(2,1)S(1)} %get-tuple-element.53), channel_id=1, source_target_pairs={{0,1},{1,0},{2,3},{3,2},{4,5},{5,4},{6,7},{7,6},{8,9},{9,8},{10,11... | collective-permute-start | bytes 516104 | tf_op jit(solution)/shard_map/ppermute | solution.py:30
  11.0 1.3 %collective-permute-start.5 = (bf16[48,1792]{1,0:T(8,128)(2,1)S(1)}, bf16[48,1792]{1,0:T(8,128)(2,1)S(1)}, u32[]{:S(2)}, u32[]{:S(2)}) collective-permute-start(bf16[48,1792]{1,0:T(8,128)(2,1)S(1)} %get-tuple-element.55), channel_id=1, source_target_pairs={{0,3},{1,2},{2,1},{3,0},{4,7},{5,6},{6,5},{7,4},{8,11},{9,10},{10,... | collective-permute-start | bytes 516104 | tf_op jit(solution)/shard_map/ppermute | solution.py:30
  12.5 1.7 %copy-done = bf16[16,128,576]{1,2,0:T(8,128)(2,1)S(1)} copy-done((bf16[16,128,576]{1,2,0:T(8,128)(2,1)S(1)}, bf16[16,128,576]{1,2,0:T(8,128)(2,1)}, u32[]{:S(2)}) %copy-start) | copy-done | bytes 2359320
  14.2 1.7 %copy-done.2 = bf16[16,128,576]{1,2,0:T(8,128)(2,1)S(1)} copy-done((bf16[16,128,576]{1,2,0:T(8,128)(2,1)S(1)}, bf16[16,128,576]{1,2,0:T(8,128)(2,1)}, u32[]{:S(2)}) %copy-start.2) | copy-done | bytes 2359320
  15.9 1.2 %shard_map.125 = (bf16[128,512]{1,0:T(8,128)(2,1)S(1)}, bf16[128,512]{1,0:T(8,128)(2,1)S(1)}, bf16[128,512]{1,0:T(8,128)(2,1)S(1)}) custom-call(s32[3]{0:T(128)S(1)} %get-tuple-element.85.index_ref, s32[3]{0:T(128)S(1)} %get-tuple-element.84.length_ref, bf16[16,576,128]{2,1,0:T(8,128)(2,1)S(1)} %bitcast.89, bf16[16,576,128]{2,1,0:T(8,128)(2,1)S(1)} %bitcast.90, ...), custom_call_target="tpu_custom_call" | custom-call | flops 106954752 | bytes 1277952 | tf_op jit(solution)/shard_map/pallas_call | solution.py:262
  17.0 1.3 %collective-permute-start.7 = (bf16[128,512]{1,0:T(8,128)(2,1)S(1)}, bf16[128,512]{1,0:T(8,128)(2,1)S(1)}, u32[]{:S(2)}, u32[]{:S(2)}) collective-permute-start(bf16[128,512]{1,0:T(8,128)(2,1)S(1)} %get-tuple-element.65), channel_id=1, source_target_pairs={{0,4},{4,0},{8,12},{12,8},{1,5},{5,1},{9,13},{13,9},{2,6},{6,2},{1... | collective-permute-start | bytes 393224 | tf_op jit(solution)/shard_map/ppermute | solution.py:30
  19.4 3.3 %shard_map.126.refs_3_ = bf16[16,128,512]{2,1,0:T(8,128)(2,1)} custom-call(s32[16]{0:T(128)S(1)} %copy-done.4, bf16[16,576,128]{2,1,0:T(8,128)(2,1)S(1)} %bitcast.92, bf16[16,576,128]{2,1,0:T(8,128)(2,1)S(1)} %bitcast.96), custom_call_target="tpu_custom_call" | custom-call | flops 570425344 | bytes 6815744 | tf_op jit(solution)/shard_map/pallas_call | solution.py:227
  23.3 3.9 %collective-permute-done.5 = bf16[48,1792]{1,0:T(8,128)(2,1)S(1)} collective-permute-done((bf16[48,1792]{1,0:T(8,128)(2,1)S(1)}, bf16[48,1792]{1,0:T(8,128)(2,1)S(1)}, u32[]{:S(2)}, u32[]{:S(2)}) %collective-permute-start.5) | collective-permute-done | bytes 172064 | tf_op jit(solution)/shard_map/ppermute | solution.py:30
  28.6 1.6 %collective-permute-start.6 = (bf16[96,1024]{1,0:T(8,128)(2,1)S(1)}, bf16[96,1024]{1,0:T(8,128)(2,1)S(1)}, u32[]{:S(2)}, u32[]{:S(2)}) collective-permute-start(bf16[96,1024]{1,0:T(8,128)(2,1)S(1)} %pad_maximum_fusion), channel_id=1, source_target_pairs={{0,4},{4,0},{8,12},{12,8},{1,5},{5,1},{9,13},{13,9},{2,6},{6,2},{1... | collective-permute-start | bytes 589832 | tf_op jit(solution)/shard_map/ppermute | solution.py:30
  32.7 1.2 %collective-permute-start.10 = (bf16[96,1024]{1,0:T(8,128)(2,1)S(1)}, bf16[96,1024]{1,0:T(8,128)(2,1)S(1)}, u32[]{:S(2)}, u32[]{:S(2)}) collective-permute-start(bf16[96,1024]{1,0:T(8,128)(2,1)S(1)} %fusion.48), channel_id=1, source_target_pairs={{0,8},{4,12},{8,0},{12,4},{1,9},{5,13},{9,1},{13,5},{2,10},{6,14},... | collective-permute-start | bytes 589832 | tf_op jit(solution)/shard_map/ppermute | solution.py:30
  34.6 1.3 %shard_map.127 = bf16[16,128,512]{2,1,0:T(8,128)(2,1)} custom-call(s32[3]{0:T(128)S(1)} %get-tuple-element.86.where_ref, bf16[128,512]{1,0:T(8,128)(2,1)S(1)} %collective-permute-done.7.refs_0_, bf16[128,512]{1,0:T(8,128)(2,1)S(1)} %collective-permute-done.8.refs_1_, ...), custom_call_target="tpu_custom_call", output_to_operand_aliasing={{}: (4, {})} | custom-call | tf_op jit(solution)/shard_map/pallas_call | solution.py:290
  36.8 2.0 %collective-permute-done.10 = bf16[96,1024]{1,0:T(8,128)(2,1)S(1)} collective-permute-done((bf16[96,1024]{1,0:T(8,128)(2,1)S(1)}, bf16[96,1024]{1,0:T(8,128)(2,1)S(1)}, u32[]{:S(2)}, u32[]{:S(2)}) %collective-permute-start.10) | collective-permute-done | bytes 196640 | tf_op jit(solution)/shard_map/ppermute | solution.py:30
  39.0 1.7 %collective-permute-start.11 = (bf16[96,512]{1,0:T(8,128)(2,1)S(1)}, bf16[96,512]{1,0:T(8,128)(2,1)S(1)}, u32[]{:S(2)}, u32[]{:S(2)}) collective-permute-start(bf16[96,512]{1,0:T(8,128)(2,1)S(1)} %fusion.72), channel_id=1, source_target_pairs={{0,4},{4,0},{8,12},{12,8},{1,5},{5,1},{9,13},{13,9},{2,6},{6,2},{1... | collective-permute-start | bytes 294920 | tf_op jit(solution)/shard_map/ppermute | solution.py:30
  42.0 1.5 %collective-permute-done.13 = bf16[96,1024]{1,0:T(8,128)(2,1)S(1)} collective-permute-done((bf16[96,1024]{1,0:T(8,128)(2,1)S(1)}, bf16[96,1024]{1,0:T(8,128)(2,1)S(1)}, u32[]{:S(2)}, u32[]{:S(2)}) %collective-permute-start.13) | collective-permute-done | bytes 196640 | tf_op jit(solution)/shard_map/ppermute | solution.py:30
  46.3 1.3 %collective-permute-start.18 = (bf16[24,1792]{1,0:T(8,128)(2,1)S(1)}, bf16[24,1792]{1,0:T(8,128)(2,1)S(1)}, u32[]{:S(2)}, u32[]{:S(2)}) collective-permute-start(bf16[24,1792]{1,0:T(8,128)(2,1)S(1)} %get-tuple-element.92), channel_id=1, source_target_pairs={{0,2},{1,3},{2,0},{3,1},{4,6},{5,7},{6,4},{7,5},{8,10},{9,11},{10,... | collective-permute-start | bytes 258056 | tf_op jit(solution)/shard_map/ppermute | solution.py:30
  47.7 1.3 %collective-permute-start.19 = (bf16[24,1792]{1,0:T(8,128)(2,1)S(1)}, bf16[24,1792]{1,0:T(8,128)(2,1)S(1)}, u32[]{:S(2)}, u32[]{:S(2)}) collective-permute-start(bf16[24,1792]{1,0:T(8,128)(2,1)S(1)} %get-tuple-element.94), channel_id=1, source_target_pairs={{0,3},{1,2},{2,1},{3,0},{4,7},{5,6},{6,5},{7,4},{8,11},{9,10},{10,... | collective-permute-start | bytes 258056 | tf_op jit(solution)/shard_map/ppermute | solution.py:30
  51.9 1.7 %collective-permute-done.18 = bf16[24,1792]{1,0:T(8,128)(2,1)S(1)} collective-permute-done((bf16[24,1792]{1,0:T(8,128)(2,1)S(1)}, bf16[24,1792]{1,0:T(8,128)(2,1)S(1)}, u32[]{:S(2)}, u32[]{:S(2)}) %collective-permute-start.18) | collective-permute-done | bytes 86048 | tf_op jit(solution)/shard_map/ppermute | solution.py:30
  53.6 6.3 %collective-permute-done.19 = bf16[24,1792]{1,0:T(8,128)(2,1)S(1)} collective-permute-done((bf16[24,1792]{1,0:T(8,128)(2,1)S(1)}, bf16[24,1792]{1,0:T(8,128)(2,1)S(1)}, u32[]{:S(2)}, u32[]{:S(2)}) %collective-permute-start.19) | collective-permute-done | bytes 86048 | tf_op jit(solution)/shard_map/ppermute | solution.py:30
  60.2 1.2 %collective-permute-start.20 = (bf16[16,1792]{1,0:T(8,128)(2,1)S(1)}, bf16[16,1792]{1,0:T(8,128)(2,1)S(1)}, u32[]{:S(2)}, u32[]{:S(2)}) collective-permute-start(bf16[16,1792]{1,0:T(8,128)(2,1)S(1)} %get-tuple-element.112), channel_id=1, source_target_pairs={{0,8},{4,12},{8,0},{12,4},{1,9},{5,13},{9,1},{13,5},{2,10},{6,14},... | collective-permute-start | bytes 172040 | tf_op jit(solution)/shard_map/ppermute | solution.py:30
  61.4 3.4 %collective-permute-start.21 = (bf16[16,1792]{1,0:T(8,128)(2,1)S(1)}, bf16[16,1792]{1,0:T(8,128)(2,1)S(1)}, u32[]{:S(2)}, u32[]{:S(2)}) collective-permute-start(bf16[16,1792]{1,0:T(8,128)(2,1)S(1)} %get-tuple-element.111), channel_id=1, source_target_pairs={{0,12},{4,8},{8,4},{12,0},{1,13},{5,9},{9,5},{13,1},{2,14},{6,10},... | collective-permute-start | bytes 172040 | tf_op jit(solution)/shard_map/ppermute | solution.py:30
  64.8 3.2 %collective-permute-done.21 = bf16[16,1792]{1,0:T(8,128)(2,1)S(1)} collective-permute-done((bf16[16,1792]{1,0:T(8,128)(2,1)S(1)}, bf16[16,1792]{1,0:T(8,128)(2,1)S(1)}, u32[]{:S(2)}, u32[]{:S(2)}) %collective-permute-start.21) | collective-permute-done | bytes 57376 | tf_op jit(solution)/shard_map/ppermute | solution.py:30
  (93 shorter events, 21.9 us)
Async XLA Ops:
  2.5 3.9 %collective-permute-start = (bf16[16,1920]{1,0:T(8,128)(2,1)}, bf16[16,1920]{1,0:T(8,128)(2,1)S(1)}, u32[]{:S(2)}, u32[]{:S(2)}) collective-permute-start(bf16[16,1920]{1,0:T(8,128)(2,1)} %get-tuple-element.44), channel_id=1, source_target_pairs={{0,4},{4,0},{8,12},{12,8},{1,5},{5,1},{9,13},{13,9},{2,6},{6,2},{1... | collective-permute-start | bytes 184328 | tf_op jit(solution)/shard_map/ppermute | solution.py:30
  3.2 3.8 %collective-permute-start.1 = (bf16[16,1920]{1,0:T(8,128)(2,1)}, bf16[16,1920]{1,0:T(8,128)(2,1)S(1)}, u32[]{:S(2)}, u32[]{:S(2)}) collective-permute-start(bf16[16,1920]{1,0:T(8,128)(2,1)} %get-tuple-element.45), channel_id=1, source_target_pairs={{0,8},{4,12},{8,0},{12,4},{1,9},{5,13},{9,1},{13,5},{2,10},{6,14},... | collective-permute-start | bytes 184328 | tf_op jit(solution)/shard_map/ppermute | solution.py:30
  4.4 4.1 %collective-permute-start.2 = (bf16[16,1920]{1,0:T(8,128)(2,1)}, bf16[16,1920]{1,0:T(8,128)(2,1)S(1)}, u32[]{:S(2)}, u32[]{:S(2)}) collective-permute-start(bf16[16,1920]{1,0:T(8,128)(2,1)} %get-tuple-element.46), channel_id=1, source_target_pairs={{0,12},{4,8},{8,4},{12,0},{1,13},{5,9},{9,5},{13,1},{2,14},{6,10},... | collective-permute-start | bytes 184328 | tf_op jit(solution)/shard_map/ppermute | solution.py:30
  9.7 13.0 %collective-permute-start.3 = (bf16[48,1792]{1,0:T(8,128)(2,1)S(1)}, bf16[48,1792]{1,0:T(8,128)(2,1)S(1)}, u32[]{:S(2)}, u32[]{:S(2)}) collective-permute-start(bf16[48,1792]{1,0:T(8,128)(2,1)S(1)} %get-tuple-element.53), channel_id=1, source_target_pairs={{0,1},{1,0},{2,3},{3,2},{4,5},{5,4},{6,7},{7,6},{8,9},{9,8},{10,11... | collective-permute-start | bytes 516104 | tf_op jit(solution)/shard_map/ppermute | solution.py:30
  11.0 12.4 %collective-permute-start.4 = (bf16[48,1792]{1,0:T(8,128)(2,1)S(1)}, bf16[48,1792]{1,0:T(8,128)(2,1)S(1)}, u32[]{:S(2)}, u32[]{:S(2)}) collective-permute-start(bf16[48,1792]{1,0:T(8,128)(2,1)S(1)} %get-tuple-element.54), channel_id=1, source_target_pairs={{0,2},{1,3},{2,0},{3,1},{4,6},{5,7},{6,4},{7,5},{8,10},{9,11},{10,... | collective-permute-start | bytes 516104 | tf_op jit(solution)/shard_map/ppermute | solution.py:30
  11.0 16.2 %collective-permute-start.5 = (bf16[48,1792]{1,0:T(8,128)(2,1)S(1)}, bf16[48,1792]{1,0:T(8,128)(2,1)S(1)}, u32[]{:S(2)}, u32[]{:S(2)}) collective-permute-start(bf16[48,1792]{1,0:T(8,128)(2,1)S(1)} %get-tuple-element.55), channel_id=1, source_target_pairs={{0,3},{1,2},{2,1},{3,0},{4,7},{5,6},{6,5},{7,4},{8,11},{9,10},{10,... | collective-permute-start | bytes 516104 | tf_op jit(solution)/shard_map/ppermute | solution.py:30
  17.0 14.3 %collective-permute-start.7 = (bf16[128,512]{1,0:T(8,128)(2,1)S(1)}, bf16[128,512]{1,0:T(8,128)(2,1)S(1)}, u32[]{:S(2)}, u32[]{:S(2)}) collective-permute-start(bf16[128,512]{1,0:T(8,128)(2,1)S(1)} %get-tuple-element.65), channel_id=1, source_target_pairs={{0,4},{4,0},{8,12},{12,8},{1,5},{5,1},{9,13},{13,9},{2,6},{6,2},{1... | collective-permute-start | bytes 393224 | tf_op jit(solution)/shard_map/ppermute | solution.py:30
  18.3 13.0 %collective-permute-start.8 = (bf16[128,512]{1,0:T(8,128)(2,1)S(1)}, bf16[128,512]{1,0:T(8,128)(2,1)S(1)}, u32[]{:S(2)}, u32[]{:S(2)}) collective-permute-start(bf16[128,512]{1,0:T(8,128)(2,1)S(1)} %get-tuple-element.66), channel_id=1, source_target_pairs={{0,8},{4,12},{8,0},{12,4},{1,9},{5,13},{9,1},{13,5},{2,10},{6,14},... | collective-permute-start | bytes 393224 | tf_op jit(solution)/shard_map/ppermute | solution.py:30
  19.4 8.8 %copy-start.6 = (bf16[1,1792,1024]{2,1,0:T(8,128)(2,1)S(1)}, bf16[1,1792,1024]{2,1,0:T(8,128)(2,1)}, u32[]{:S(2)}) copy-start(bf16[1,1792,1024]{2,1,0:T(8,128)(2,1)} %param.20) | copy-start | bytes 11010052
  22.6 8.7 %collective-permute-start.9 = (bf16[128,512]{1,0:T(8,128)(2,1)S(1)}, bf16[128,512]{1,0:T(8,128)(2,1)S(1)}, u32[]{:S(2)}, u32[]{:S(2)}) collective-permute-start(bf16[128,512]{1,0:T(8,128)(2,1)S(1)} %get-tuple-element.67), channel_id=1, source_target_pairs={{0,12},{4,8},{8,4},{12,0},{1,13},{5,9},{9,5},{13,1},{2,14},{6,10},... | collective-permute-start | bytes 393224 | tf_op jit(solution)/shard_map/ppermute | solution.py:30
  28.6 2.7 %collective-permute-start.6 = (bf16[96,1024]{1,0:T(8,128)(2,1)S(1)}, bf16[96,1024]{1,0:T(8,128)(2,1)S(1)}, u32[]{:S(2)}, u32[]{:S(2)}) collective-permute-start(bf16[96,1024]{1,0:T(8,128)(2,1)S(1)} %pad_maximum_fusion), channel_id=1, source_target_pairs={{0,4},{4,0},{8,12},{12,8},{1,5},{5,1},{9,13},{13,9},{2,6},{6,2},{1... | collective-permute-start | bytes 589832 | tf_op jit(solution)/shard_map/ppermute | solution.py:30
  32.7 6.2 %collective-permute-start.10 = (bf16[96,1024]{1,0:T(8,128)(2,1)S(1)}, bf16[96,1024]{1,0:T(8,128)(2,1)S(1)}, u32[]{:S(2)}, u32[]{:S(2)}) collective-permute-start(bf16[96,1024]{1,0:T(8,128)(2,1)S(1)} %fusion.48), channel_id=1, source_target_pairs={{0,8},{4,12},{8,0},{12,4},{1,9},{5,13},{9,1},{13,5},{2,10},{6,14},... | collective-permute-start | bytes 589832 | tf_op jit(solution)/shard_map/ppermute | solution.py:30
  33.9 2.5 %collective-permute-start.12 = (bf16[96,1024]{1,0:T(8,128)(2,1)S(1)}, bf16[96,1024]{1,0:T(8,128)(2,1)S(1)}, u32[]{:S(2)}, u32[]{:S(2)}) collective-permute-start(bf16[96,1024]{1,0:T(8,128)(2,1)S(1)} %pad_maximum_fusion.1), channel_id=1, source_target_pairs={{0,4},{4,0},{8,12},{12,8},{1,5},{5,1},{9,13},{13,9},{2,6},{6,2},{1... | collective-permute-start | bytes 589832 | tf_op jit(solution)/shard_map/ppermute | solution.py:30
  36.4 7.0 %collective-permute-start.13 = (bf16[96,1024]{1,0:T(8,128)(2,1)S(1)}, bf16[96,1024]{1,0:T(8,128)(2,1)S(1)}, u32[]{:S(2)}, u32[]{:S(2)}) collective-permute-start(bf16[96,1024]{1,0:T(8,128)(2,1)S(1)} %fusion.49), channel_id=1, source_target_pairs={{0,8},{4,12},{8,0},{12,4},{1,9},{5,13},{9,1},{13,5},{2,10},{6,14},... | collective-permute-start | bytes 589832 | tf_op jit(solution)/shard_map/ppermute | solution.py:30
  39.0 2.6 %collective-permute-start.11 = (bf16[96,512]{1,0:T(8,128)(2,1)S(1)}, bf16[96,512]{1,0:T(8,128)(2,1)S(1)}, u32[]{:S(2)}, u32[]{:S(2)}) collective-permute-start(bf16[96,512]{1,0:T(8,128)(2,1)S(1)} %fusion.72), channel_id=1, source_target_pairs={{0,4},{4,0},{8,12},{12,8},{1,5},{5,1},{9,13},{13,9},{2,6},{6,2},{1... | collective-permute-start | bytes 294920 | tf_op jit(solution)/shard_map/ppermute | solution.py:30
  43.6 1.8 %collective-permute-start.14 = (bf16[96,512]{1,0:T(8,128)(2,1)S(1)}, bf16[96,512]{1,0:T(8,128)(2,1)S(1)}, u32[]{:S(2)}, u32[]{:S(2)}) collective-permute-start(bf16[96,512]{1,0:T(8,128)(2,1)S(1)} %fusion.71), channel_id=1, source_target_pairs={{0,4},{4,0},{8,12},{12,8},{1,5},{5,1},{9,13},{13,9},{2,6},{6,2},{1... | collective-permute-start | bytes 294920 | tf_op jit(solution)/shard_map/ppermute | solution.py:30
  46.2 5.7 %collective-permute-start.15 = (bf16[48,1792]{1,0:T(8,128)(2,1)S(1)}, bf16[48,1792]{1,0:T(8,128)(2,1)S(1)}, u32[]{:S(2)}, u32[]{:S(2)}) collective-permute-start(bf16[48,1792]{1,0:T(8,128)(2,1)S(1)} %pad_maximum_fusion.2), channel_id=1, source_target_pairs={{0,1},{1,0},{2,3},{3,2},{4,5},{5,4},{6,7},{7,6},{8,9},{9,8},{10,11... | collective-permute-start | bytes 516104 | tf_op jit(solution)/shard_map/ppermute | solution.py:30
  46.3 7.2 %collective-permute-start.18 = (bf16[24,1792]{1,0:T(8,128)(2,1)S(1)}, bf16[24,1792]{1,0:T(8,128)(2,1)S(1)}, u32[]{:S(2)}, u32[]{:S(2)}) collective-permute-start(bf16[24,1792]{1,0:T(8,128)(2,1)S(1)} %get-tuple-element.92), channel_id=1, source_target_pairs={{0,2},{1,3},{2,0},{3,1},{4,6},{5,7},{6,4},{7,5},{8,10},{9,11},{10,... | collective-permute-start | bytes 258056 | tf_op jit(solution)/shard_map/ppermute | solution.py:30
  47.7 12.2 %collective-permute-start.19 = (bf16[24,1792]{1,0:T(8,128)(2,1)S(1)}, bf16[24,1792]{1,0:T(8,128)(2,1)S(1)}, u32[]{:S(2)}, u32[]{:S(2)}) collective-permute-start(bf16[24,1792]{1,0:T(8,128)(2,1)S(1)} %get-tuple-element.94), channel_id=1, source_target_pairs={{0,3},{1,2},{2,1},{3,0},{4,7},{5,6},{6,5},{7,4},{8,11},{9,10},{10,... | collective-permute-start | bytes 258056 | tf_op jit(solution)/shard_map/ppermute | solution.py:30
  49.0 15.9 %collective-permute-start.16 = (bf16[24,1792]{1,0:T(8,128)(2,1)S(1)}, bf16[24,1792]{1,0:T(8,128)(2,1)S(1)}, u32[]{:S(2)}, u32[]{:S(2)}) collective-permute-start(bf16[24,1792]{1,0:T(8,128)(2,1)S(1)} %get-tuple-element.96), channel_id=1, source_target_pairs={{0,2},{1,3},{2,0},{3,1},{4,6},{5,7},{6,4},{7,5},{8,10},{9,11},{10,... | collective-permute-start | bytes 258056 | tf_op jit(solution)/shard_map/ppermute | solution.py:30
  50.0 14.9 %collective-permute-start.17 = (bf16[24,1792]{1,0:T(8,128)(2,1)S(1)}, bf16[24,1792]{1,0:T(8,128)(2,1)S(1)}, u32[]{:S(2)}, u32[]{:S(2)}) collective-permute-start(bf16[24,1792]{1,0:T(8,128)(2,1)S(1)} %get-tuple-element.95), channel_id=1, source_target_pairs={{0,3},{1,2},{2,1},{3,0},{4,7},{5,6},{6,5},{7,4},{8,11},{9,10},{10,... | collective-permute-start | bytes 258056 | tf_op jit(solution)/shard_map/ppermute | solution.py:30
  60.2 4.6 %collective-permute-start.20 = (bf16[16,1792]{1,0:T(8,128)(2,1)S(1)}, bf16[16,1792]{1,0:T(8,128)(2,1)S(1)}, u32[]{:S(2)}, u32[]{:S(2)}) collective-permute-start(bf16[16,1792]{1,0:T(8,128)(2,1)S(1)} %get-tuple-element.112), channel_id=1, source_target_pairs={{0,8},{4,12},{8,0},{12,4},{1,9},{5,13},{9,1},{13,5},{2,10},{6,14},... | collective-permute-start | bytes 172040 | tf_op jit(solution)/shard_map/ppermute | solution.py:30
  61.4 6.6 %collective-permute-start.21 = (bf16[16,1792]{1,0:T(8,128)(2,1)S(1)}, bf16[16,1792]{1,0:T(8,128)(2,1)S(1)}, u32[]{:S(2)}, u32[]{:S(2)}) collective-permute-start(bf16[16,1792]{1,0:T(8,128)(2,1)S(1)} %get-tuple-element.111), channel_id=1, source_target_pairs={{0,12},{4,8},{8,4},{12,0},{1,13},{5,9},{9,5},{13,1},{2,14},{6,10},... | collective-permute-start | bytes 172040 | tf_op jit(solution)/shard_map/ppermute | solution.py:30
  68.4 1.5 %collective-permute-start.22 = (bf16[16,1792]{1,0:T(8,128)(2,1)S(1)}, bf16[16,1792]{1,0:T(8,128)(2,1)S(1)}, u32[]{:S(2)}, u32[]{:S(2)}) collective-permute-start(bf16[16,1792]{1,0:T(8,128)(2,1)S(1)} %get-tuple-element.109), channel_id=1, source_target_pairs={{0,4},{4,0},{8,12},{12,8},{1,5},{5,1},{9,13},{13,9},{2,6},{6,2},{1... | collective-permute-start | bytes 172040 | tf_op jit(solution)/shard_map/ppermute | solution.py:30
  (8 other events, 21.6 us)
